TPU v7x, 512 devices: a whole 4x8x8 slice. The times are simulated.
512 devices in a mesh: grid: 64 (over z, y), rep: 8 (over x, core).
Axes of the slice: x: 4, y: 8, z: 8, core: 2. Of those that a mesh axis runs over, the one named last changes fastest.
Arguments:
- b_tensor: bfloat16 [8, 1024, 8192], P('rep', 'grid'), may hold values from -6 to 6
- green_occ: bfloat16 [8, 1024, 1024], P('rep', 'grid'), may hold values from -0.1875 to 0.1875
- green_vir: bfloat16 [8, 1024, 1024], P('rep', 'grid'), may hold values from -0.1875 to 0.1875
- b_pattern: int32 [8, 16, 16], P('rep'), may hold values 0 or 1
- g_pattern: int32 [8, 16, 16], P('rep'), may hold values 0 or 1
Outputs:
- occ_tensor: bfloat16 [8, 1024, 8192], P('rep', None, 'grid')
- vir_tensor: bfloat16 [8, 1024, 8192], P('rep', 'grid')
- chi: float32 [8, 8], replicated
All inputs are finite; a program needn't handle non-finite values. No bound on the sum of `b_pattern` or of `g_pattern` on one device may be relied on, other than what follows from the above.
Results may differ from a plain program's by a relative error of at most 0.0056.
Values may be sent and summed in bfloat16 or wider, within the bound.
A program may use at most 64 MiB of HBM per device.

v0:
```python
import math

import jax
import jax.numpy as jnp
from jax import lax
from jax.sharding import PartitionSpec as P

BS = 64


def molecule_hot(indices, molecules):
    return (indices[:, None] // BS == jnp.arange(molecules)[None, :]).astype(jnp.float32)


def per_device(b_tensor, green_occ, green_vir, b_pattern, g_pattern):
    rows_local = b_tensor.shape[1]
    merged = b_tensor.shape[2]
    rows_all = green_occ.shape[2]
    functions = merged // rows_all
    molecules = b_pattern.shape[1]
    position = lax.axis_index("grid")
    full_hot = molecule_hot(jnp.arange(rows_all), molecules)
    strip_hot = molecule_hot(position * rows_local + jnp.arange(rows_local), molecules)
    tensor_mask = jnp.dot(jnp.dot(strip_hot, b_pattern[0].astype(jnp.float32)), full_hot.T).astype(
        jnp.bfloat16
    )
    blocks = b_tensor[0].reshape(rows_local, rows_all, functions) * tensor_mask[:, :, None]
    green_mask = jnp.dot(jnp.dot(strip_hot, g_pattern[0].astype(jnp.float32)), full_hot.T).astype(
        jnp.bfloat16
    )
    occ_piece = green_occ[0] * green_mask
    vir_piece = green_vir[0] * green_mask
    flattened = blocks.reshape(rows_local, merged)
    occ_full, vir_full = (
        lax.all_gather(occ_piece, "grid", axis=0, tiled=True),
        lax.all_gather(vir_piece, "grid", axis=0, tiled=True),
    )
    vir_rows = jnp.einsum("lsq,sn->lnq", blocks, vir_full, preferred_element_type=jnp.float32)
    vir_flat = vir_rows.astype(jnp.bfloat16).reshape(rows_local, merged)
    tensor_cols, vir_cols = (
        lax.all_to_all(flattened, "grid", split_axis=1, concat_axis=0, tiled=True),
        lax.all_to_all(vir_flat, "grid", split_axis=1, concat_axis=0, tiled=True),
    )
    occ_cols = jnp.dot(occ_full, tensor_cols, preferred_element_type=jnp.float32).astype(
        jnp.bfloat16
    )
    chi_part = lax.dot_general(
        occ_cols.reshape(-1, functions),
        vir_cols.reshape(-1, functions),
        (((0,), (0,)), ((), ())),
        preferred_element_type=jnp.float32,
    )
    scale = -1.0 / (rows_all * math.sqrt(lax.axis_size("rep")))
    chi = lax.psum(chi_part, ("grid", "rep")) * scale
    return (occ_cols[None], vir_flat[None], chi)


def solution(mesh):
    return jax.shard_map(
        per_device,
        mesh=mesh,
        in_specs=(
            P("rep", "grid", None),
            P("rep", "grid", None),
            P("rep", "grid", None),
            P("rep", None, None),
            P("rep", None, None),
        ),
        out_specs=(P("rep", None, "grid"), P("rep", "grid", None), P()),
        check_vma=False,
    )
```

profile of v0, /device:TPU:1, one launch (start us, length us, event | category | flops | bytes accessed | tf_op | source)
XLA Modules:
  0.0 307.8 jit_solution(7024578123450554444)
XLA Ops:
  7.2 0.0 all-gather.5.cloned.1.call-start
  7.2 1.7 bitcast_multiply_fusion.2
  9.0 0.0 all-gather.5.cloned.1.call-update
  9.0 0.0 all-gather.3.cloned.1.call-start
  9.1 0.7 all-gather.3.cloned.1.call-update
  9.8 1.0 convolution_convert_fusion.1
  10.8 0.2 copy.19
  11.0 1.9 copy.18
  12.9 0.3 mul.31
  13.2 1.5 bitcast_multiply_fusion.1
  14.7 2.5 copy.20
  17.2 17.1 %all-to-all-start = ((bf16[16,64,128]{2,0,1:T(8,128)(2,1)}), bf16[16,64,128]{2,0,1:T(8,128)(2,1)S(1)}, u32[]{:S(2)}, u32[]{:S(2)}) async-start(bf16[16,64,128]{2,0,1:T(8,128)(2,1)} %copy.20), calls=%async_computation | async-start | bytes 524288 | tf_op jit(solution)/shard_map/all_to_all | solution.py:41
  34.3 1.6 bitcast_multiply_fusion
  35.9 62.2 %all-gather.5.cloned.1.call-done = bf16[1024,1024]{1,0:T(8,128)(2,1)} async-done(((bf16[16,1024]{1,0:T(8,128)(2,1)}), bf16[1024,1024]{1,0:T(8,128)(2,1)}) %all-gather.5.cloned.1.call-update) | async-done | bytes 2097168 | tf_op jit(solution)/shard_map/all_gather | solution.py:36
  98.2 3.0 fusion.8
  101.2 1.6 copy.23
  102.8 1.4 copy.25
  104.2 0.0 all-to-all-done
  104.2 8.4 %all-to-all-start.1 = ((bf16[16,64,128]{2,0,1:T(8,128)(2,1)}), bf16[16,64,128]{2,0,1:T(8,128)(2,1)S(1)}, u32[]{:S(2)}, u32[]{:S(2)}) async-start(bf16[16,64,128]{2,0,1:T(8,128)(2,1)} %copy.25), calls=%async_computation.1 | async-start | bytes 524288 | tf_op jit(solution)/shard_map/all_to_all | solution.py:42
  112.6 1.4 copy.26
  114.1 68.8 %all-gather.3.cloned.1.call-done = bf16[1024,1024]{1,0:T(8,128)(2,1)} async-done(((bf16[16,1024]{1,0:T(8,128)(2,1)}), bf16[1024,1024]{1,0:T(8,128)(2,1)}) %all-gather.3.cloned.1.call-update) | async-done | bytes 2097168 | tf_op jit(solution)/shard_map/all_gather | solution.py:35
  182.8 2.3 convolution_convert_fusion
  185.1 0.0 copy-start
  185.1 5.8 %reshape.103 = bf16[16384,8]{1,0:T(8,128)(2,1)} reshape(bf16[1024,128]{1,0:T(8,128)(2,1)S(1)} %convolution_convert_fusion) | data formatting | bytes 524288 | tf_op jit(solution)/shard_map/reshape | solution.py:48
  190.9 0.0 copy-done
  190.9 0.0 all-to-all-done.1
  190.9 5.8 %reshape.104 = bf16[16384,8]{1,0:T(8,128)(2,1)} reshape(bf16[64,16,128]{2,1,0:T(8,128)(2,1)S(1)} %bitcast.46) | data formatting | bytes 524288 | tf_op jit(solution)/shard_map/reshape | solution.py:49
  196.7 4.7 %fusion.36 = f32[8,8]{1,0:T(8,128)S(1)} fusion(bf16[16384,8]{1,0:T(8,128)(2,1)} %reshape.103, bf16[16384,8]{1,0:T(8,128)(2,1)} %reshape.104), kind=kOutput, calls=%fused_computation.36 | convolution fusion | flops 2097152 | bytes 524544 | tf_op jit(solution)/shard_map/dot_general | solution.py:47
  201.3 99.0 %psum.7 = f32[8,8]{1,0:T(8,128)S(1)} all-reduce(f32[8,8]{1,0:T(8,128)S(1)} %fusion.36), channel_id=1, replica_groups=mesh['grid'=64,'rep'=8] {'grid','rep'}, use_global_device_ids=true, to_apply=%region_0.1 | all-reduce | flops 64 | bytes 512 | tf_op jit(solution)/shard_map/psum | solution.py:54
  300.4 0.6 broadcast_multiply_fusion
  (2 shorter events, 0.0 us)
Async XLA Ops:
  7.2 91.0 %all-gather.5.cloned.1.call-start = ((), (), s32[]{:S(2)}) async-start(), calls=%async_computation.3 | async-start | bytes 2129920 | tf_op jit(solution)/shard_map/all_gather | solution.py:36
  9.0 173.8 %all-gather.3.cloned.1.call-start = ((), (), s32[]{:S(2)}) async-start(), calls=%async_computation.2 | async-start | bytes 2129920 | tf_op jit(solution)/shard_map/all_gather | solution.py:35
  17.2 87.0 %all-to-all-start = ((bf16[16,64,128]{2,0,1:T(8,128)(2,1)}), bf16[16,64,128]{2,0,1:T(8,128)(2,1)S(1)}, u32[]{:S(2)}, u32[]{:S(2)}) async-start(bf16[16,64,128]{2,0,1:T(8,128)(2,1)} %copy.20), calls=%async_computation | async-start | bytes 524288 | tf_op jit(solution)/shard_map/all_to_all | solution.py:41
  104.2 86.7 %all-to-all-start.1 = ((bf16[16,64,128]{2,0,1:T(8,128)(2,1)}), bf16[16,64,128]{2,0,1:T(8,128)(2,1)S(1)}, u32[]{:S(2)}, u32[]{:S(2)}) async-start(bf16[16,64,128]{2,0,1:T(8,128)(2,1)} %copy.25), calls=%async_computation.1 | async-start | bytes 524288 | tf_op jit(solution)/shard_map/all_to_all | solution.py:42
  185.1 5.8 %copy-start = (bf16[1024,128]{1,0:T(8,128)(2,1)}, bf16[1024,128]{1,0:T(8,128)(2,1)S(1)}, u32[]{:S(2)}) copy-start(bf16[1024,128]{1,0:T(8,128)(2,1)S(1)} %convolution_convert_fusion) | copy-start | bytes 786436
Sparse Core Ops, SparseCore 0:
  11.6 86.4 all-gather.4
  101.2 81.5 all-gather.2
where the time goes:
time: 308 us
  waiting for transfers between devices  132 us (43%)
  blocking collectives  99 us (32%)
  starting transfers between devices  25.6 us (8%)
  local copies, waits for them, and re-layouts  20.9 us (7%)
  between operations  14.1 us (5%)
  matrix products  12.7 us (4%)
  other arithmetic  3.73 us (1%)
    psum x1, blocking collectives, per_device(): chi = lax.psum(chi_part, ('grid', 'rep')) * scale  99 us
    all_gather x1, waiting for transfers between devices, per_device(): lax.all_gather(occ_piece, 'grid', axis=0, tiled=True)  68.8 us
    all_gather x1, waiting for transfers between devices, per_device(): lax.all_gather(vir_piece, 'grid', axis=0, tiled=True)  62.2 us
    all_to_all x1, starting transfers between devices, per_device(): lax.all_to_all(flattened, 'grid', split_axis=1, concat_axis=0, tiled=True)  17.1 us
    all_to_all x1, starting transfers between devices, per_device(): lax.all_to_all(vir_flat, 'grid', split_axis=1, concat_axis=0, tiled=True)  8.4 us
  transfers between devices with their start and end apart: 4, of which 2 were waited for; matrix products, arithmetic and copies ran while one was open for 8% of the time, Pallas kernels for 0%

commit v1 on v0

v1 whole, which is shorter than its diff:
```python
import functools
import math

import jax
import jax.numpy as jnp
from jax import lax
from jax.experimental import pallas as pl
from jax.experimental.pallas import tpu as pltpu
from jax.sharding import PartitionSpec as P

MESH = pl.DeviceIdType.MESH
SIDE = 8
ROWS = 16
ORBS = 1024
RB = 8
TILE = ROWS * RB
WIDE = SIDE * TILE
CHUNK = SIDE * ROWS
HALF = CHUNK // 2
ITEMS = 7
F32 = jnp.float32
BF16 = jnp.bfloat16


def around(index, step):
    return lax.rem(index + (step + SIDE), SIDE)


def kernel(
    scale,
    b_ref,
    occ_ref,
    vir_ref,
    bp_ref,
    gp_ref,
    occ_out,
    vir_out,
    chi_out,
    green,
    spread,
    middle,
    landed,
    columns,
    perm,
    left_side,
    total,
    mixed,
    shares,
    one_send,
    one_recv,
    ring_send,
    ring_recv,
    swap_send,
    swap_recv,
    chi_send,
    chi_recv,
):
    grid_ix = lax.axis_index("grid")
    rep_ix = lax.axis_index("rep")
    z, y = grid_ix // SIDE, grid_ix % SIDE
    core = rep_ix % 2
    a0 = z + core * (y - z)
    b0 = y + core * (z - y)
    sa = SIDE - (SIDE - 1) * core
    sb = 1 + (SIDE - 1) * core

    def nat(a, b):
        return a * sa + b * sb

    def at(a, b):
        return (nat(a, b), rep_ix)

    def remote(src, dst, send, recv, where):
        return pltpu.make_async_remote_copy(
            src_ref=src, dst_ref=dst, send_sem=send, recv_sem=recv, device_id=where, device_id_type=MESH
        )

    barrier = pltpu.get_barrier_semaphore()

    def greet(i, carry):
        for where in (at(around(a0, i), b0), at(a0, around(b0, i)), (grid_ix, around(rep_ix, i))):
            pl.semaphore_signal(barrier, inc=1, device_id=where, device_id_type=MESH)
        return carry

    lax.fori_loop(1, SIDE, greet, 0)

    molecule = grid_ix // 4
    lane = lax.broadcasted_iota(jnp.int32, (ROWS, 128), 1)
    me = a0 * SIDE + b0
    for t in range(SIDE):
        lo = gp_ref[0, molecule, 2 * t]
        hi = gp_ref[0, molecule, 2 * t + 1]
        keep = jnp.where(lane < 64, lo, hi).astype(F32).astype(BF16)
        cols = slice(t * 128, (t + 1) * 128)
        green[0, me, :, cols] = vir_ref[0, :, cols] * keep
        green[1, me, :, cols] = occ_ref[0, :, cols] * keep

    def lay(a, carry):
        for b in range(SIDE):
            n = nat(a, b)
            keep = jnp.full((ROWS, TILE), bp_ref[0, molecule, n // 4], jnp.int32).astype(F32).astype(BF16)
            tile = b_ref[0, :, pl.ds(pl.multiple_of(n * TILE, TILE), TILE)]
            spread[0, a, :, b * TILE : (b + 1) * TILE] = tile * keep
        return carry

    lax.fori_loop(0, SIDE, lay, 0)

    pl.semaphore_wait(barrier, 3 * (SIDE - 1))

    def first(which):
        def body(i, carry):
            block = green.at[which, me]
            remote(block, block, one_send.at[which], one_recv.at[which], at(a0, around(b0, i))).start()
            return carry

        lax.fori_loop(1, SIDE, body, 0)

    def first_done(which):
        seven = green.at[which, pl.ds(0, SIDE - 1)]
        remote(seven, seven, one_send.at[which], one_recv.at[which], at(a0, around(b0, 1))).wait()

    def swap_a(which):
        def body(i, carry):
            a = around(a0, i)
            remote(
                spread.at[which, a],
                middle.at[which, a0],
                swap_send.at[which, 0],
                swap_recv.at[which, 0],
                at(a, b0),
            ).start()
            return carry

        lax.fori_loop(1, SIDE, body, 0)
        middle[which, a0] = spread[which, a0]

    def swap_a_done(which):
        seven = middle.at[which, pl.ds(0, SIDE - 1)]
        remote(seven, seven, swap_send.at[which, 0], swap_recv.at[which, 0], at(around(a0, 1), b0)).wait()

    def tile_of(b):
        return pl.ds(pl.multiple_of(b * TILE, TILE), TILE)

    def swap_b(which):
        def body(i, carry):
            b = around(b0, i)
            remote(
                middle.at[which, :, :, tile_of(b)],
                landed.at[which, b0],
                swap_send.at[which, 1],
                swap_recv.at[which, 1],
                at(a0, b),
            ).start()
            return carry

        lax.fori_loop(1, SIDE, body, 0)
        landed[which, b0] = middle[which, :, :, tile_of(b0)]

    def swap_b_done(which):
        seven = landed.at[which, pl.ds(0, SIDE - 1)]
        remote(seven, seven, swap_send.at[which, 1], swap_recv.at[which, 1], at(a0, around(b0, 1))).wait()

        def body(b, carry):
            for a in range(SIDE):
                row = pl.multiple_of(nat(a, b) * ROWS, ROWS)
                columns[which, pl.ds(row, ROWS), :] = landed[which, b, a]
            return carry

        lax.fori_loop(0, SIDE, body, 0)

    def ring(which, way, item):
        step = item // 2
        half = (item % 2) if way == 0 else 1 - (item % 2)
        sign = 1 if way == 0 else -1
        begin = around(a0, -sign * step) * SIDE + half * (SIDE // 2)
        block = green.at[which, pl.ds(begin, SIDE // 2)]
        return remote(
            block, block, ring_send.at[which, way, item], ring_recv.at[which, way, item], at(around(a0, sign), b0)
        )

    def ring_arrival(which, way, item):
        step = item // 2 + 1
        half = (item % 2) if way == 0 else 1 - (item % 2)
        sign = 1 if way == 0 else -1
        begin = around(a0, -sign * step) * SIDE + half * (SIDE // 2)
        block = green.at[which, pl.ds(begin, SIDE // 2)]
        return remote(
            block, block, ring_send.at[which, way, item], ring_recv.at[which, way, item], at(around(a0, sign), b0)
        )

    def ring_start(which):
        for item in range(2):
            for way in range(2):
                ring(which, way, item).start()

    def ring_step(which, item):
        for way in range(2):
            ring_arrival(which, way, item).wait_recv()
            if item + 2 < ITEMS:
                ring(which, way, item + 2).start()

    def ring_drain(which):
        for item in range(ITEMS):
            for way in range(2):
                ring(which, way, item).wait_send()

    def add_vir(a):
        chunk = green[0, pl.ds(a * SIDE, SIDE)].reshape(CHUNK, ORBS)
        total[...] += jnp.dot(left_side[a], chunk, preferred_element_type=F32)

    def put_occ(a):
        chunk = green[1, pl.ds(a * SIDE, SIDE)].reshape(CHUNK, ORBS)
        part = jnp.dot(chunk, columns[0], preferred_element_type=F32).astype(BF16)
        for b in range(SIDE):
            row = pl.multiple_of(nat(a, b) * ROWS, ROWS)
            occ_out[0, pl.ds(row, ROWS), :] = part[b * ROWS : (b + 1) * ROWS]

    first(0)
    swap_a(0)
    first(1)

    target = lax.broadcasted_iota(jnp.int32, (256, WIDE), 1)
    target = (target % 128) * RB + target // 128

    def fill(i, carry):
        row = lax.broadcasted_iota(jnp.int32, (256, WIDE), 0) + i * 256
        perm[pl.ds(pl.multiple_of(i * 256, 256), 256), :] = jnp.where(row == target, 1.0, 0.0).astype(BF16)
        return carry

    lax.fori_loop(0, WIDE // 256, fill, 0)
    total[...] = jnp.zeros_like(total)
    apart = jnp.dot(
        spread[0].reshape(CHUNK, WIDE), perm[...], preferred_element_type=F32
    ).astype(BF16)
    for a in range(SIDE):
        for q in range(RB):
            left_side[a, q * ROWS : (q + 1) * ROWS, :] = apart[a * ROWS : (a + 1) * ROWS, q * 128 : (q + 1) * 128]

    first_done(0)
    ring_start(0)
    swap_a_done(0)
    swap_b(0)
    add_vir(a0)
    first_done(1)
    for item in range(ITEMS):
        ring_step(0, item)
        if item == 3:
            ring_start(1)
        if item % 2 == 1:
            step = item // 2 + 1
            add_vir(around(a0, -step))
            add_vir(around(a0, step))
        elif item == ITEMS - 1:
            add_vir(around(a0, SIDE // 2))

    for c in range(SIDE):
        for q in range(RB):
            mixed[c * ROWS : (c + 1) * ROWS, q * 128 : (q + 1) * 128] = total[
                q * ROWS : (q + 1) * ROWS, c * 128 : (c + 1) * 128
            ].astype(BF16)
    merged = lax.dot_general(
        mixed[...], perm[...], (((1,), (1,)), ((), ())), preferred_element_type=F32
    ).astype(BF16)
    for c in range(SIDE):
        vir_out[0, :, c * WIDE : (c + 1) * WIDE] = merged[c * ROWS : (c + 1) * ROWS]

    def lay_vir(a, carry):
        for b in range(SIDE):
            spread[1, a, :, b * TILE : (b + 1) * TILE] = vir_out[0, :, tile_of(nat(a, b))]
        return carry

    lax.fori_loop(0, SIDE, lay_vir, 0)
    swap_a(1)

    swap_b_done(0)
    put_occ(a0)
    for item in range(ITEMS):
        ring_step(1, item)
        if item % 2 == 1:
            step = item // 2 + 1
            put_occ(around(a0, -step))
            put_occ(around(a0, step))
        elif item == ITEMS - 1:
            put_occ(around(a0, SIDE // 2))
        if item == 3:
            swap_a_done(1)
            swap_b(1)
    swap_b_done(1)

    gram = lax.dot_general(
        occ_out[0], columns[1], (((0,), (0,)), ((), ())), preferred_element_type=F32
    )
    row = lax.broadcasted_iota(jnp.int32, (TILE, TILE), 0)
    col = lax.broadcasted_iota(jnp.int32, (TILE, TILE), 1)
    gram = jnp.where(row // RB == col // RB, gram, 0.0)
    share = jnp.sum(gram.reshape(ROWS, RB, TILE), axis=0)
    for shift in (8, 16, 32, 64):
        share = share + pltpu.roll(share, shift, 1)

    def exchange(stage, mine, where, value):
        shares[stage, mine] = value

        def body(i, carry):
            block = shares.at[stage, mine]
            remote(block, block, chi_send.at[stage], chi_recv.at[stage], where(i)).start()
            return carry

        lax.fori_loop(1, SIDE, body, 0)
        seven = shares.at[stage, pl.ds(0, SIDE - 1)]
        remote(seven, seven, chi_send.at[stage], chi_recv.at[stage], where(1)).wait()
        return jnp.sum(shares[stage], axis=0)

    share = exchange(0, a0, lambda i: at(around(a0, i), b0), share)
    share = exchange(1, b0, lambda i: at(a0, around(b0, i)), share)
    share = exchange(2, rep_ix, lambda i: (grid_ix, around(rep_ix, i)), share)
    chi_out[...] = share[:, :RB] * scale
    ring_drain(0)
    ring_drain(1)


def per_device(b_tensor, green_occ, green_vir, b_pattern, g_pattern):
    scale = -1.0 / (ORBS * math.sqrt(lax.axis_size("rep")))
    vmem = pl.BlockSpec(memory_space=pltpu.VMEM)
    smem = pl.BlockSpec(memory_space=pltpu.SMEM)
    return pl.pallas_call(
        functools.partial(kernel, scale),
        out_shape=(
            jax.ShapeDtypeStruct((1, ORBS, TILE), BF16),
            jax.ShapeDtypeStruct((1, ROWS, ORBS * RB), BF16),
            jax.ShapeDtypeStruct((RB, RB), F32),
        ),
        in_specs=[vmem, vmem, vmem, smem, smem],
        out_specs=(vmem, vmem, vmem),
        scratch_shapes=[
            pltpu.VMEM((2, SIDE * SIDE, ROWS, ORBS), BF16),
            pltpu.VMEM((2, SIDE, ROWS, WIDE), BF16),
            pltpu.VMEM((2, SIDE, ROWS, WIDE), BF16),
            pltpu.VMEM((2, SIDE, SIDE, ROWS, TILE), BF16),
            pltpu.VMEM((2, ORBS, TILE), BF16),
            pltpu.VMEM((WIDE, WIDE), BF16),
            pltpu.VMEM((SIDE, CHUNK, 128), BF16),
            pltpu.VMEM((CHUNK, ORBS), F32),
            pltpu.VMEM((CHUNK, ORBS), BF16),
            pltpu.VMEM((3, SIDE, RB, TILE), F32),
            pltpu.SemaphoreType.DMA((2,)),
            pltpu.SemaphoreType.DMA((2,)),
            pltpu.SemaphoreType.DMA((2, 2, ITEMS)),
            pltpu.SemaphoreType.DMA((2, 2, ITEMS)),
            pltpu.SemaphoreType.DMA((2, 2)),
            pltpu.SemaphoreType.DMA((2, 2)),
            pltpu.SemaphoreType.DMA((3,)),
            pltpu.SemaphoreType.DMA((3,)),
        ],
        compiler_params=pltpu.CompilerParams(
            collective_id=0, has_side_effects=True, vmem_limit_bytes=40 * 1024 * 1024
        ),
        cost_estimate=pl.CostEstimate(flops=600_000_000, bytes_accessed=1_200_000, transcendentals=0),
    )(b_tensor, green_occ, green_vir, b_pattern, g_pattern)


def solution(mesh):
    return jax.shard_map(
        per_device,
        mesh=mesh,
        in_specs=(
            P("rep", "grid", None),
            P("rep", "grid", None),
            P("rep", "grid", None),
            P("rep", None, None),
            P("rep", None, None),
        ),
        out_specs=(P("rep", None, "grid"), P("rep", "grid", None), P()),
        check_vma=False,
    )
```

time: 308 us -> 85.1 us (0.28)
  waiting for transfers between devices: 132 us -> 0 us
  blocking collectives: 99 us -> 0 us
  Pallas kernels: 0 us -> 78.2 us
  starting transfers between devices: 25.6 us -> 0 us
  local copies, waits for them, and re-layouts: 20.9 us -> 5.85 us
  between operations: 14.1 us -> 0.65 us
  matrix products: 12.7 us -> 0 us
  other arithmetic: 3.73 us -> 0 us
    all_gather x2 -> x0, waiting for transfers between devices: 131 us -> none  [the longest x1 68.8 us: per_device(): lax.all_gather(occ_piece, 'grid', axis=0, tiled=True)]
    psum x1 -> x0, blocking collectives: 99 us -> none  [per_device(): chi = lax.psum(chi_part, ('grid', 'rep')) * scale]
    pallas_call x0 -> x1, Pallas kernels: none -> 78.2 us  [per_device(): pl.pallas_call(functools.partial(kernel, scale), out_shape=(jax.ShapeDtyp...]
    all_to_all x2 -> x0, starting transfers between devices: 25.5 us -> none  [the longest x1 17.1 us: per_device(): lax.all_to_all(flattened, 'grid', split_axis=1, concat_axis=0, tiled=True)]
    dot_general x5 -> x0, matrix products: 12.7 us -> none  [the longest x1 4.69 us: per_device(): lax.dot_general(occ_cols.reshape(-1, functions), vir_cols.reshape(-1, fun...]
    reshape x2 -> x0, local copies, waits for them, and re-layouts: 11.5 us -> none  [the longest x1 5.76 us: per_device(): occ_cols.reshape(-1, functions)]
    mul x3 -> x0, other arithmetic: 3.72 us -> none  [the longest x2 3.12 us: per_device(): b_tensor[0].reshape(rows_local, rows_all, functions)]
  transfers between devices with their start and end apart: 4 -> 0, of which waited for: 2 -> 0; matrix products, arithmetic and copies ran while one was open for 8% -> 0% of each run, Pallas kernels for 0% -> 0%
where the time goes in v1:
time: 85.1 us; the launch traced here: 84.7 us
  Pallas kernels  78.2 us (92%)
  local copies, waits for them, and re-layouts  5.85 us (7%)
    pallas_call x1, Pallas kernels, per_device(): pl.pallas_call(functools.partial(kernel, scale), out_shape=(jax.ShapeDtyp...  78.2 us
    unnamed x13, local copies, waits for them, and re-layouts  5.85 us

profile of v1, /device:TPU:1, one launch (start us, length us, event | category | flops | bytes accessed | tf_op | source)
XLA Modules:
  0.0 84.7 jit_solution(1898425997906417464)
XLA Ops:
  0.6 0.0 copy-start
  0.6 0.9 %copy-done = bf16[1,16,8192]{2,1,0:T(8,128)(2,1)S(1)} copy-done((bf16[1,16,8192]{2,1,0:T(8,128)(2,1)S(1)}, bf16[1,16,8192]{2,1,0:T(8,128)(2,1)}, u32[]{:S(2)}) %copy-start) | copy-done | bytes 262168
  1.6 0.0 copy-start.1
  1.6 0.8 copy-done.1
  2.3 0.0 copy-start.2
  2.3 0.8 copy-done.2
  3.1 0.0 copy-start.3
  3.1 0.7 copy-done.3
  3.8 0.0 copy-start.4
  3.8 0.7 copy-done.4
  4.5 78.2 %shard_map.76 = (bf16[1,1024,128]{2,1,0:T(8,128)(2,1)S(1)}, bf16[1,16,8192]{2,1,0:T(8,128)(2,1)S(1)}, f32[8,8]{1,0:T(8,128)S(1)}) custom-call(bf16[1,16,8192]{2,1,0:T(8,128)(2,1)S(1)} %copy-done, bf16[1,16,1024]{2,1,0:T(8,128)(2,1)S(1)} %copy-done.1, bf16[1,16,1024]{2,1,0:T(8,128)(2,1)S(1)} %copy-done.2, s32[1,16,16]{2,1,0:T(8,128)S(1)} %copy-done.3, ...), custom_call_target="tpu_custom_call" | custom-call | flops 600000000 | bytes 1200000 | tf_op jit(solution)/shard_map/pallas_call | solution.py:325
  82.7 0.7 copy.11
  83.4 0.7 copy.12
  84.2 0.6 copy.13
Async XLA Ops:
  0.6 1.0 %copy-start = (bf16[1,16,8192]{2,1,0:T(8,128)(2,1)S(1)}, bf16[1,16,8192]{2,1,0:T(8,128)(2,1)}, u32[]{:S(2)}) copy-start(bf16[1,16,8192]{2,1,0:T(8,128)(2,1)} %b_ref.1) | copy-start | bytes 786436
  1.6 0.8 copy-start.1
  2.3 0.8 copy-start.2
  3.1 0.7 copy-start.3
  3.8 0.7 copy-start.4

commit v2 on v0

v2 whole, which is shorter than its diff:
```python
import functools
import math

import jax
import jax.numpy as jnp
from jax import lax
from jax.experimental import pallas as pl
from jax.experimental.pallas import tpu as pltpu
from jax.sharding import PartitionSpec as P

MESH = pl.DeviceIdType.MESH
SIDE = 8
PLANE = SIDE * SIDE
HALF = SIDE // 2
ROWS = 16
ORBS = 1024
RB = 8
TILE = ROWS * RB
WIDE = SIDE * TILE
F32 = jnp.float32
BF16 = jnp.bfloat16


def around(index, step):
    return lax.rem(index + (step + SIDE), SIDE)


def kernel(
    scale,
    b_hbm,
    occ_hbm,
    vir_hbm,
    bp_hbm,
    gp_hbm,
    occ_out,
    vir_out,
    chi_out,
    b_ref,
    occ_ref,
    vir_ref,
    bp_ref,
    gp_ref,
    vir_own,
    vir_all,
    occ_all,
    spread,
    other,
    middle,
    landed,
    landed_two,
    both,
    perm,
    sort,
    left_side,
    total,
    mixed,
    merged,
    vir_land,
    vir_back,
    occ_own,
    occ_two,
    occ_back,
    shares,
    shares_rep,
    io_sem,
    vir_one_send,
    vir_one_recv,
    occ_one_send,
    occ_one_recv,
    vir_ring_send,
    vir_ring_recv,
    occ_ring_send,
    occ_ring_recv,
    swap_send,
    swap_recv,
    pair_send,
    pair_recv,
    chi_send,
    chi_recv,
):
    grid_ix = lax.axis_index("grid")
    rep_ix = lax.axis_index("rep")
    z, y = grid_ix // SIDE, grid_ix % SIDE
    core = rep_ix % 2
    a0 = z + core * (y - z)
    b0 = y + core * (z - y)
    sa = SIDE - (SIDE - 1) * core
    sb = 1 + (SIDE - 1) * core
    par = b0 % 2
    jb = b0 // 2
    vir_mate = around(b0, 2 * par - 1)
    occ_mate = around(b0, 1 - 2 * par)

    def nat(a, b):
        return a * sa + b * sb

    def at(a, b):
        return (nat(a, b), rep_ix)

    def remote(src, dst, send, recv, where):
        return pltpu.make_async_remote_copy(
            src_ref=src, dst_ref=dst, send_sem=send, recv_sem=recv, device_id=where, device_id_type=MESH
        )

    def tile_of(i):
        return pl.ds(pl.multiple_of(i * TILE, TILE), TILE)

    def rows_of(i):
        return pl.ds(pl.multiple_of(i * ROWS, ROWS), ROWS)

    barrier = pltpu.get_barrier_semaphore()

    def greet(i, carry):
        for where in (at(around(a0, i), b0), at(a0, around(b0, i)), (grid_ix, around(rep_ix, i))):
            pl.semaphore_signal(barrier, inc=1, device_id=where, device_id_type=MESH)
        return carry

    lax.fori_loop(1, SIDE, greet, 0)

    loads = [
        pltpu.make_async_copy(src, dst, io_sem.at[i])
        for i, (src, dst) in enumerate(
            ((gp_hbm, gp_ref), (vir_hbm, vir_ref), (bp_hbm, bp_ref), (b_hbm, b_ref), (occ_hbm, occ_ref))
        )
    ]
    for load in loads:
        load.start()

    def fill_sort(i, carry):
        m = lax.broadcasted_iota(jnp.int32, (256, ORBS), 1)
        a, b = (m // ROWS) % SIDE, 2 * ((m // 128) % HALF) + m // 512
        source = (a * sa + b * sb) * ROWS + m % ROWS
        row = lax.broadcasted_iota(jnp.int32, (256, ORBS), 0) + i * 256
        sort[pl.ds(pl.multiple_of(i * 256, 256), 256), :] = jnp.where(row == source, 1.0, 0.0).astype(BF16)
        return carry

    lax.fori_loop(0, ORBS // 256, fill_sort, 0)

    molecule = grid_ix // 4
    lane = lax.broadcasted_iota(jnp.int32, (ROWS, 128), 1)
    loads[0].wait()
    loads[1].wait()
    keeps = [
        jnp.where(lane < 64, gp_ref[0, molecule, 2 * t], gp_ref[0, molecule, 2 * t + 1]).astype(F32).astype(BF16)
        for t in range(SIDE)
    ]
    for t in range(SIDE):
        cols = slice(t * 128, (t + 1) * 128)
        vir_ref[0, :, cols] = vir_ref[0, :, cols] * keeps[t]
    sorted_vir = jnp.dot(vir_ref[0], sort[...], preferred_element_type=F32).astype(BF16)
    vir_own[0] = sorted_vir[:, :512]
    vir_own[1] = sorted_vir[:, 512:]
    vir_all[a0 * SIDE + b0] = vir_own[par]

    loads[2].wait()
    loads[3].wait()

    def lay(a, carry):
        for b in range(SIDE):
            n = nat(a, b)
            keep = jnp.full((ROWS, TILE), bp_ref[0, molecule, n // 4], jnp.int32).astype(F32).astype(BF16)
            spread[a, :, b * TILE : (b + 1) * TILE] = b_ref[0, :, tile_of(n)] * keep
        return carry

    lax.fori_loop(0, SIDE, lay, 0)
    loads[4].wait()
    for t in range(SIDE):
        cols = slice(t * 128, (t + 1) * 128)
        occ_all[a0 * HALF + jb, :, cols] = occ_ref[0, :, cols] * keeps[t]

    pl.semaphore_wait(barrier, 3 * (SIDE - 1))

    def near(k):
        return ((k + 1) // 2) * (2 * (k % 2) - 1)

    def vir_block(a, k):
        return vir_all.at[a * SIDE + around(b0, near(k))]

    def occ_block(a, k):
        return occ_all.at[a * HALF + around(b0, 2 * near(k)) // 2]

    def vir_one(b):
        return remote(
            vir_own.at[b % 2], vir_all.at[a0 * SIDE + b0], vir_one_send.at[b], vir_one_recv.at[b0], at(a0, b)
        )

    def vir_one_arrival(b):
        block = vir_all.at[a0 * SIDE + b]
        return remote(block, block, vir_one_send.at[b], vir_one_recv.at[b], at(a0, b))

    def occ_one(b):
        block = occ_all.at[a0 * HALF + jb]
        return remote(block, block, occ_one_send.at[b // 2], occ_one_recv.at[jb], at(a0, b))

    def occ_one_arrival(b):
        block = occ_all.at[a0 * HALF + b // 2]
        return remote(block, block, occ_one_send.at[b // 2], occ_one_recv.at[b // 2], at(a0, b))

    def hop(block, send, recv, way, d, k):
        sign = 1 - 2 * way
        piece = block(around(a0, -sign * (d - 1)), k)
        return remote(piece, piece, send.at[way, d - 1, k], recv.at[way, d - 1, k], at(around(a0, sign), b0))

    def arrival(block, send, recv, way, d, k):
        sign = 1 - 2 * way
        piece = block(around(a0, -sign * d), k)
        return remote(piece, piece, send.at[way, d - 1, k], recv.at[way, d - 1, k], at(around(a0, sign), b0))

    vir_ring = (vir_block, vir_ring_send, vir_ring_recv)
    occ_ring = (occ_block, occ_ring_send, occ_ring_recv)

    def ring_begin(ring, count, one_arrival, stride):
        def body(k, carry):
            one_arrival(around(b0, stride * near(k))).wait_recv()
            hop(*ring, 0, 1, k).start()
            hop(*ring, 1, 1, k).start()
            return carry

        hop(*ring, 0, 1, 0).start()
        hop(*ring, 1, 1, 0).start()
        lax.fori_loop(1, count, body, 0)

    def ring_step(ring, count, d):
        def body(low, high, k, carry):
            if d < 4 or low:
                arrival(*ring, 0, d, k).wait_recv()
                if d < 3 or (d == 3 and low):
                    hop(*ring, 0, d + 1, k).start()
            if d < 4 or high:
                arrival(*ring, 1, d, k).wait_recv()
                if d < 3 or (d == 3 and high):
                    hop(*ring, 1, d + 1, k).start()
            return carry

        lax.fori_loop(0, count // 2, functools.partial(body, True, False), 0)
        lax.fori_loop(count // 2, count, functools.partial(body, False, True), 0)

    def ring_drain(ring, count):
        def body(low, k, carry):
            for d in range(1, 4):
                hop(*ring, 0, d, k).wait_send()
                hop(*ring, 1, d, k).wait_send()
            hop(*ring, 0 if low else 1, 4, k).wait_send()
            return carry

        lax.fori_loop(0, count // 2, functools.partial(body, True), 0)
        lax.fori_loop(count // 2, count, functools.partial(body, False), 0)

    def vir_one_start(i, carry):
        vir_one(around(b0, i)).start()
        return carry

    lax.fori_loop(1, SIDE, vir_one_start, 0)

    def swap_a(i, carry):
        a = around(a0, i)
        remote(spread.at[a], middle.at[a0], swap_send.at[0], swap_recv.at[0], at(a, b0)).start()
        return carry

    def swap_b(i, carry):
        b = around(b0, i)
        remote(
            middle.at[:, :, tile_of(b)], landed.at[b0], swap_send.at[1], swap_recv.at[1], at(a0, b)
        ).start()
        return carry

    pair_spread = remote(spread, other, pair_send.at[0], pair_recv.at[0], at(a0, vir_mate))
    pair_landed = remote(landed, landed_two, pair_send.at[1], pair_recv.at[1], at(a0, occ_mate))
    pair_vir = remote(
        merged.at[pl.ds(PLANE, PLANE)], vir_back, pair_send.at[2], pair_recv.at[2], at(a0, vir_mate)
    )
    pair_occ = remote(occ_two, occ_back, pair_send.at[3], pair_recv.at[3], at(a0, occ_mate))

    lax.fori_loop(1, SIDE, swap_a, 0)
    middle[a0] = spread[a0]
    pair_spread.start()
    for step in (2, 6, 4):
        occ_one(around(b0, step)).start()

    target = lax.broadcasted_iota(jnp.int32, (256, WIDE), 1)
    target = (target % 128) * RB + target // 128

    def fill(i, carry):
        row = lax.broadcasted_iota(jnp.int32, (256, WIDE), 0) + i * 256
        perm[pl.ds(pl.multiple_of(i * 256, 256), 256), :] = jnp.where(row == target, 1.0, 0.0).astype(BF16)
        return carry

    def part(w, source):
        apart = jnp.dot(source[...].reshape(128, WIDE), perm[...], preferred_element_type=F32).astype(BF16)
        for a in range(SIDE):
            for q in range(RB):
                row = w * 128 + q * ROWS
                left_side[a, row : row + ROWS, :] = apart[a * ROWS : (a + 1) * ROWS, q * 128 : (q + 1) * 128]

    def add_vir(a):
        chunk = vir_all[pl.ds(a * SIDE, SIDE)].reshape(128, 512)
        total[...] += jnp.dot(left_side[a], chunk, preferred_element_type=F32)

    def put_occ(a):
        chunk = occ_all[pl.ds(a * HALF, HALF)].reshape(64, ORBS)
        product = jnp.dot(chunk, both[...], preferred_element_type=F32).astype(BF16)
        rows = pl.ds(pl.multiple_of(a * 64, 64), 64)
        occ_own[rows, :] = product[:, :TILE]
        occ_two[rows, :] = product[:, TILE:]

    ring_begin(vir_ring, SIDE, vir_one_arrival, 1)
    lax.fori_loop(0, WIDE // 256, fill, 0)
    total[...] = jnp.zeros_like(total)
    part(0, spread)
    ring_begin(occ_ring, HALF, occ_one_arrival, 2)

    ring_step(vir_ring, SIDE, 1)

    seven = middle.at[pl.ds(0, SIDE - 1)]
    remote(seven, seven, swap_send.at[0], swap_recv.at[0], at(around(a0, 1), b0)).wait()
    lax.fori_loop(1, SIDE, swap_b, 0)
    landed[b0] = middle[:, :, tile_of(b0)]
    pair_spread.wait()
    part(1, other)
    add_vir(a0)

    ring_step(occ_ring, HALF, 1)
    ring_step(vir_ring, SIDE, 2)
    add_vir(around(a0, -1))
    add_vir(around(a0, 1))
    ring_step(occ_ring, HALF, 2)
    ring_step(vir_ring, SIDE, 3)
    add_vir(around(a0, -2))
    add_vir(around(a0, 2))

    seven = landed.at[pl.ds(0, SIDE - 1)]
    remote(seven, seven, swap_send.at[1], swap_recv.at[1], at(a0, around(b0, 1))).wait()
    pair_landed.start()

    ring_step(occ_ring, HALF, 3)
    add_vir(around(a0, -3))
    add_vir(around(a0, 3))
    ring_step(vir_ring, SIDE, 4)
    add_vir(around(a0, 4))

    for w in range(2):
        for j in range(HALF):
            for q in range(RB):
                row, new = (w * RB + q) * ROWS, (w * HALF + j) * ROWS
                mixed[new : new + ROWS, q * 128 : (q + 1) * 128] = total[
                    row : row + ROWS, j * 128 : (j + 1) * 128
                ].astype(BF16)
    merged[...] = lax.dot_general(
        mixed[...], perm[...], (((1,), (1,)), ((), ())), preferred_element_type=F32
    ).astype(BF16)

    def vir_own_swap(i, carry):
        a, j = around(a0, i // HALF), (jb + i) % HALF
        remote(
            merged.at[rows_of(j), tile_of(a)],
            vir_land.at[a0 * HALF + jb],
            swap_send.at[2],
            swap_recv.at[2],
            at(a, 2 * j + par),
        ).start()
        return carry

    def vir_mate_swap(i, carry):
        a, j = around(a0, i // HALF), (jb + i) % HALF
        remote(
            merged.at[rows_of(HALF + j), tile_of(a)],
            vir_land.at[PLANE // 2 + a0 * HALF + vir_mate // 2],
            swap_send.at[2],
            swap_recv.at[2],
            at(a, around(2 * j + par, 1 - 2 * par)),
        ).start()
        return carry

    lax.fori_loop(1, PLANE // 2, vir_own_swap, 0)
    lax.fori_loop(0, PLANE // 2, vir_mate_swap, 0)
    vir_land[a0 * HALF + jb] = merged[rows_of(jb), tile_of(a0)]
    pair_vir.start()

    pair_landed.wait()

    def join(b, carry):
        for a in range(SIDE):
            rows = rows_of(nat(a, b))
            both[rows, :TILE] = landed[b, a]
            both[rows, TILE:] = landed_two[b, a]
        return carry

    lax.fori_loop(0, SIDE, join, 0)
    put_occ(a0)
    for d in range(1, 4):
        put_occ(around(a0, -d))
        put_occ(around(a0, d))
    ring_step(occ_ring, HALF, 4)
    put_occ(around(a0, 4))
    pair_occ.start()

    most = vir_land.at[pl.ds(0, PLANE - 1)]
    remote(most, most, swap_send.at[2], swap_recv.at[2], at(a0, around(b0, 1))).wait()

    gram = jnp.zeros((TILE, TILE), F32)
    for c, mine in enumerate((occ_own, occ_two)):
        theirs = vir_land[c * PLANE // 2 : (c + 1) * PLANE // 2].reshape(512, TILE)
        gram += lax.dot_general(mine[...], theirs, (((0,), (0,)), ((), ())), preferred_element_type=F32)
    row = lax.broadcasted_iota(jnp.int32, (TILE, TILE), 0)
    col = lax.broadcasted_iota(jnp.int32, (TILE, TILE), 1)
    gram = jnp.where(row // RB == col // RB, gram, 0.0)
    share = jnp.sum(gram.reshape(ROWS, RB, TILE), axis=0)

    def fold(values):
        for shift in (8, 16, 32, 64):
            values = values + pltpu.roll(values, shift, 1)
        return values

    place = lax.broadcasted_iota(jnp.int32, (RB, TILE), 1) // RB == lax.broadcasted_iota(jnp.int32, (RB, TILE), 0)
    share = jnp.sum(jnp.where(place, fold(share), 0.0), axis=0, keepdims=True)

    shares[pl.ds(grid_ix, 1), :] = share

    def tell(i, carry):
        line = shares.at[pl.ds(grid_ix, 1)]
        remote(line, line, chi_send.at[0], chi_recv.at[0], (lax.rem(grid_ix + i, PLANE), rep_ix)).start()
        return carry

    lax.fori_loop(1, PLANE, tell, 0)
    for a in range(SIDE):
        for j in range(HALF):
            vir_out[0, :, tile_of(nat(a, 2 * j + par))] = merged[j * ROWS : (j + 1) * ROWS, a * TILE : (a + 1) * TILE]
            occ_out[0, rows_of(nat(a, 2 * j + par)), :] = occ_own[(a * HALF + j) * ROWS : (a * HALF + j + 1) * ROWS]
    pair_vir.wait()
    for a in range(SIDE):
        for j in range(HALF):
            vir_out[0, :, tile_of(nat(a, 2 * j + 1 - par))] = vir_back[
                j * ROWS : (j + 1) * ROWS, a * TILE : (a + 1) * TILE
            ]
    pair_occ.wait()
    for a in range(SIDE):
        for j in range(HALF):
            occ_out[0, rows_of(nat(a, 2 * j + 1 - par)), :] = occ_back[
                (a * HALF + j) * ROWS : (a * HALF + j + 1) * ROWS
            ]
    ring_drain(vir_ring, SIDE)
    ring_drain(occ_ring, HALF)

    def vir_one_drain(i, carry):
        vir_one(around(b0, i)).wait_send()
        return carry

    lax.fori_loop(1, SIDE, vir_one_drain, 0)
    for step in (2, 6, 4):
        occ_one(around(b0, step)).wait_send()

    lines = shares.at[pl.ds(0, PLANE - 1)]
    remote(lines, lines, chi_send.at[0], chi_recv.at[0], at(a0, around(b0, 1))).wait()
    shares_rep[pl.ds(rep_ix, 1), :] = jnp.sum(shares[...], axis=0, keepdims=True)

    def tell_rep(i, carry):
        line = shares_rep.at[pl.ds(rep_ix, 1)]
        remote(line, line, chi_send.at[1], chi_recv.at[1], (grid_ix, around(rep_ix, i))).start()
        return carry

    lax.fori_loop(1, SIDE, tell_rep, 0)
    lines = shares_rep.at[pl.ds(0, SIDE - 1)]
    remote(lines, lines, chi_send.at[1], chi_recv.at[1], (grid_ix, around(rep_ix, 1))).wait()
    share = jnp.sum(shares_rep[...], axis=0, keepdims=True) * scale
    share = fold(jnp.where(place, jnp.broadcast_to(share, (RB, TILE)), 0.0))
    chi_out[...] = share[:, :RB]


def per_device(b_tensor, green_occ, green_vir, b_pattern, g_pattern):
    scale = -1.0 / (ORBS * math.sqrt(lax.axis_size("rep")))
    vmem = pl.BlockSpec(memory_space=pltpu.VMEM)
    hbm = pl.BlockSpec(memory_space=pltpu.HBM)
    dma = pltpu.SemaphoreType.DMA
    return pl.pallas_call(
        functools.partial(kernel, scale),
        out_shape=(
            jax.ShapeDtypeStruct((1, ORBS, TILE), BF16),
            jax.ShapeDtypeStruct((1, ROWS, ORBS * RB), BF16),
            jax.ShapeDtypeStruct((RB, RB), F32),
        ),
        in_specs=[hbm] * 5,
        out_specs=(vmem, vmem, vmem),
        scratch_shapes=[
            pltpu.VMEM(b_tensor.shape, BF16),
            pltpu.VMEM(green_occ.shape, BF16),
            pltpu.VMEM(green_vir.shape, BF16),
            pltpu.SMEM(b_pattern.shape, jnp.int32),
            pltpu.SMEM(g_pattern.shape, jnp.int32),
            pltpu.VMEM((2, ROWS, 512), BF16),
            pltpu.VMEM((PLANE, ROWS, 512), BF16),
            pltpu.VMEM((PLANE // 2, ROWS, ORBS), BF16),
            pltpu.VMEM((SIDE, ROWS, WIDE), BF16),
            pltpu.VMEM((SIDE, ROWS, WIDE), BF16),
            pltpu.VMEM((SIDE, ROWS, WIDE), BF16),
            pltpu.VMEM((SIDE, SIDE, ROWS, TILE), BF16),
            pltpu.VMEM((SIDE, SIDE, ROWS, TILE), BF16),
            pltpu.VMEM((ORBS, 2 * TILE), BF16),
            pltpu.VMEM((WIDE, WIDE), BF16),
            pltpu.VMEM((ORBS, ORBS), BF16),
            pltpu.VMEM((SIDE, 256, 128), BF16),
            pltpu.VMEM((256, 512), F32),
            pltpu.VMEM((128, WIDE), BF16),
            pltpu.VMEM((128, WIDE), BF16),
            pltpu.VMEM((PLANE, ROWS, TILE), BF16),
            pltpu.VMEM((PLANE, WIDE), BF16),
            pltpu.VMEM((512, TILE), BF16),
            pltpu.VMEM((512, TILE), BF16),
            pltpu.VMEM((512, TILE), BF16),
            pltpu.VMEM((PLANE, TILE), F32),
            pltpu.VMEM((SIDE, TILE), F32),
            dma((5,)),
            dma((SIDE,)),
            dma((SIDE,)),
            dma((HALF,)),
            dma((HALF,)),
            dma((2, 4, SIDE)),
            dma((2, 4, SIDE)),
            dma((2, 4, HALF)),
            dma((2, 4, HALF)),
            dma((3,)),
            dma((3,)),
            dma((4,)),
            dma((4,)),
            dma((2,)),
            dma((2,)),
        ],
        compiler_params=pltpu.CompilerParams(
            collective_id=0, has_side_effects=True, vmem_limit_bytes=56 * 1024 * 1024
        ),
        cost_estimate=pl.CostEstimate(flops=600_000_000, bytes_accessed=1_200_000, transcendentals=0),
    )(b_tensor, green_occ, green_vir, b_pattern, g_pattern)


def solution(mesh):
    return jax.shard_map(
        per_device,
        mesh=mesh,
        in_specs=(
            P("rep", "grid", None),
            P("rep", "grid", None),
            P("rep", "grid", None),
            P("rep", None, None),
            P("rep", None, None),
        ),
        out_specs=(P("rep", None, "grid"), P("rep", "grid", None), P()),
        check_vma=False,
    )
```

time: 308 us -> 70 us (0.23)
  waiting for transfers between devices: 132 us -> 0 us
  blocking collectives: 99 us -> 0 us
  Pallas kernels: 0 us -> 66.1 us
  starting transfers between devices: 25.6 us -> 0 us
  local copies, waits for them, and re-layouts: 20.9 us -> 3.01 us
  between operations: 14.1 us -> 0.65 us
  matrix products: 12.7 us -> 0 us
  other arithmetic: 3.73 us -> 0 us
    all_gather x2 -> x0, waiting for transfers between devices: 131 us -> none  [the longest x1 68.8 us: per_device(): lax.all_gather(occ_piece, 'grid', axis=0, tiled=True)]
    psum x1 -> x0, blocking collectives: 99 us -> none  [per_device(): chi = lax.psum(chi_part, ('grid', 'rep')) * scale]
    pallas_call x0 -> x1, Pallas kernels: none -> 66.1 us  [per_device(): pl.pallas_call(functools.partial(kernel, scale), out_shape=(jax.ShapeDtyp...]
    all_to_all x2 -> x0, starting transfers between devices: 25.5 us -> none  [the longest x1 17.1 us: per_device(): lax.all_to_all(flattened, 'grid', split_axis=1, concat_axis=0, tiled=True)]
    dot_general x5 -> x0, matrix products: 12.7 us -> none  [the longest x1 4.69 us: per_device(): lax.dot_general(occ_cols.reshape(-1, functions), vir_cols.reshape(-1, fun...]
    reshape x2 -> x0, local copies, waits for them, and re-layouts: 11.5 us -> none  [the longest x1 5.76 us: per_device(): occ_cols.reshape(-1, functions)]
    mul x3 -> x0, other arithmetic: 3.72 us -> none  [the longest x2 3.12 us: per_device(): b_tensor[0].reshape(rows_local, rows_all, functions)]
  transfers between devices with their start and end apart: 4 -> 0, of which waited for: 2 -> 0; matrix products, arithmetic and copies ran while one was open for 8% -> 0% of each run, Pallas kernels for 0% -> 0%
where the time goes in v2:
time: 70 us; the launch traced here: 69.8 us
  Pallas kernels  66.1 us (94%)
  local copies, waits for them, and re-layouts  3.01 us (4%)
    pallas_call x1, Pallas kernels, per_device(): pl.pallas_call(functools.partial(kernel, scale), out_shape=(jax.ShapeDtyp...  66.1 us
    unnamed x7, local copies, waits for them, and re-layouts  3.01 us

profile of v2, /device:TPU:1, one launch (start us, length us, event | category | flops | bytes accessed | tf_op | source)
XLA Modules:
  0.0 69.8 jit_solution(8821666898896626396)
XLA Ops:
  0.6 66.1 %shard_map.76 = (bf16[1,1024,128]{2,1,0:T(8,128)(2,1)}, bf16[1,16,8192]{2,1,0:T(8,128)(2,1)}, f32[8,8]{1,0:T(8,128)}) custom-call(bf16[1,16,8192]{2,1,0:T(8,128)(2,1)} %b_hbm.1, bf16[1,16,1024]{2,1,0:T(8,128)(2,1)} %occ_hbm.1, bf16[1,16,1024]{2,1,0:T(8,128)(2,1)} %vir_hbm.1, s32[1,16,16]{2,1,0:T(8,128)} %bp_hbm.1, s32[1,16,16]{2,1,0:T(8,128)} %gp_hbm.1), custom_call_target="tpu_custom_call" | custom-call | flops 600000000 | bytes 1200000 | tf_op jit(solution)/shard_map/pallas_call | solution.py:474
  66.8 0.0 copy-start
  66.8 1.7 %copy.11 = bf16[1,1024,128]{2,1,0:T(8,128)(2,1)} copy(bf16[1,1024,128]{2,1,0:T(8,128)(2,1)} %get-tuple-element.6) | data formatting | bytes 524288
  68.5 0.0 copy-done
  68.5 0.0 copy-start.1
  68.5 0.7 %copy.12 = bf16[1,16,8192]{2,1,0:T(8,128)(2,1)} copy(bf16[1,16,8192]{2,1,0:T(8,128)(2,1)S(1)} %copy-done) | data formatting | bytes 524288
  69.2 0.0 copy-done.1
  69.2 0.6 copy.13
Async XLA Ops:
  66.8 1.7 %copy-start = (bf16[1,16,8192]{2,1,0:T(8,128)(2,1)S(1)}, bf16[1,16,8192]{2,1,0:T(8,128)(2,1)}, u32[]{:S(2)}) copy-start(bf16[1,16,8192]{2,1,0:T(8,128)(2,1)} %get-tuple-element.7) | copy-start | bytes 786436
  68.5 0.7 %copy-start.1 = (f32[8,8]{1,0:T(8,128)S(1)}, f32[8,8]{1,0:T(8,128)}, u32[]{:S(2)}) copy-start(f32[8,8]{1,0:T(8,128)} %get-tuple-element.8) | copy-start | bytes 772

commit v3 on v0

v3 whole, which is shorter than its diff:
```python
import functools
import math

import jax
import jax.numpy as jnp
from jax import lax
from jax.experimental import pallas as pl
from jax.experimental.pallas import tpu as pltpu
from jax.sharding import PartitionSpec as P

MESH = pl.DeviceIdType.MESH
SIDE = 8
PLANE = SIDE * SIDE
HALF = SIDE // 2
ROWS = 16
ORBS = 1024
RB = 8
TILE = ROWS * RB
WIDE = SIDE * TILE
F32 = jnp.float32
BF16 = jnp.bfloat16


def around(index, step):
    return lax.rem(index + (step + SIDE), SIDE)


FAR = [4, 5, 3, 6, 2, 7, 1]
SUBS = 4


def kernel(
    scale,
    b_hbm,
    occ_hbm,
    vir_hbm,
    bp_hbm,
    gp_hbm,
    occ_out,
    vir_out,
    chi_out,
    b_ref,
    occ_ref,
    vir_ref,
    bp_ref,
    gp_ref,
    vir_own,
    vir_all,
    occ_all,
    strips,
    left_side,
    landed,
    both,
    perm,
    mixed,
    merged,
    vir_land,
    vir_back,
    occ_pair,
    occ_two,
    occ_back,
    shares,
    shares_rep,
    io_sem,
    vir_send,
    vir_recv,
    occ_one_send,
    occ_one_recv,
    occ_ring_send,
    occ_ring_recv,
    strip_send,
    strip_recv,
    swap_send,
    swap_recv,
    chi_send,
    chi_recv,
):
    grid_ix = lax.axis_index("grid")
    rep_ix = lax.axis_index("rep")
    z, y = grid_ix // SIDE, grid_ix % SIDE
    core = rep_ix % 2
    a0 = z + core * (y - z)
    b0 = y + core * (z - y)
    sa = SIDE - (SIDE - 1) * core
    sb = 1 + (SIDE - 1) * core
    par = b0 % 2
    jb = b0 // 2
    mate = around(b0, 1 - 2 * par)
    abs_a = [around(a0, i) for i in range(SIDE)]
    abs_b = [around(b0, j) for j in range(SIDE)]
    part_a = [a * sa for a in abs_a]
    part_b = [b * sb for b in abs_b]

    def nat(i, j):
        return part_a[i % SIDE] + part_b[j % SIDE]

    def at(i, j):
        return (nat(i, j), rep_ix)

    def at_mate(i):
        return (part_a[i % SIDE] + mate * sb, rep_ix)

    def remote(src, dst, send, recv, where):
        return pltpu.make_async_remote_copy(
            src_ref=src, dst_ref=dst, send_sem=send, recv_sem=recv, device_id=where, device_id_type=MESH
        )

    def send(*copy):
        remote(*copy).start()

    def tile_of(i):
        return pl.ds(pl.multiple_of(i * TILE, TILE), TILE)

    def rows_of(i, count=ROWS):
        return pl.ds(pl.multiple_of(i * count, count), count)

    barrier = pltpu.get_barrier_semaphore()
    for i in range(1, SIDE):
        for where in (at(i, 0), at(0, i), (grid_ix, around(rep_ix, i))):
            pl.semaphore_signal(barrier, inc=1, device_id=where, device_id_type=MESH)

    loads = [
        pltpu.make_async_copy(src, dst, io_sem.at[i])
        for i, (src, dst) in enumerate(
            ((gp_hbm, gp_ref), (vir_hbm, vir_ref), (bp_hbm, bp_ref), (b_hbm, b_ref), (occ_hbm, occ_ref))
        )
    ]
    for load in loads:
        load.start()

    molecule = grid_ix // 4
    lane = lax.broadcasted_iota(jnp.int32, (ROWS, 128), 1)
    loads[0].wait()
    loads[1].wait()
    keeps = [
        jnp.where(lane < 64, gp_ref[0, molecule, 2 * t], gp_ref[0, molecule, 2 * t + 1]).astype(F32)
        for t in range(SIDE)
    ]
    tiles = [vir_ref[0, :, t * 128 : (t + 1) * 128].astype(F32) * keeps[t] for t in range(SIDE)]
    for bit in (1, 2, 4):
        high = (lane // ROWS // bit) % 2 + 2 * core
        for t in range(SIDE):
            if t & bit == 0:
                u = t + bit
                low_tile = jnp.where(high == 1, pltpu.roll(tiles[u], ROWS * bit, 1), tiles[t])
                high_tile = jnp.where(high == 0, pltpu.roll(tiles[t], 128 - ROWS * bit, 1), tiles[u])
                tiles[t], tiles[u] = low_tile, high_tile
    for b in range(SIDE):
        vir_own[b] = tiles[b].astype(BF16)
    vir_all[0, b0] = vir_own[b0]

    loads[2].wait()
    loads[3].wait()
    for m in range(2 * SIDE):
        keep = jnp.full((ROWS, 512), bp_ref[0, molecule, m], jnp.int32).astype(F32).astype(BF16)
        cols = slice(m * 512, (m + 1) * 512)
        b_ref[0, :, cols] = b_ref[0, :, cols] * keep
    for i in range(SIDE):
        for b in range(SIDE):
            strips[0, i, :, b * TILE : (b + 1) * TILE] = b_ref[0, :, tile_of(part_a[i] + b * sb)]
    loads[4].wait()
    for t in range(SIDE):
        cols = slice(t * 128, (t + 1) * 128)
        occ_all[0, 0, :, cols] = occ_ref[0, :, cols] * keeps[t].astype(BF16)

    pl.semaphore_wait(barrier, 3 * (SIDE - 1))

    for j in FAR:
        send(vir_own.at[abs_b[j]], vir_all.at[0, b0], vir_send.at[0], vir_recv.at[0], at(0, j))

    def strip_ring(way, d, u):
        sign = 1 - 2 * way
        send(
            strips.at[-sign * (d - 1) % SIDE, pl.ds(2 * u, 2)],
            strips.at[-sign * d % SIDE, pl.ds(2 * u, 2)],
            strip_send,
            strip_recv.at[way, SUBS * (d - 1) + u % (SUBS if d < 4 else SUBS // 2)],
            at(0, sign),
        )

    def strip_wait(way, d, u):
        piece = strips.at[(2 * way - 1) * d % SIDE, pl.ds(2 * u, 2)]
        slot = strip_recv.at[way, SUBS * (d - 1) + u % (SUBS if d < 4 else SUBS // 2)]
        remote(piece, piece, strip_send, slot, at(0, 1)).wait_recv()

    def occ_ring(way, d, g):
        sign = 1 - 2 * way
        send(
            occ_all.at[-sign * (d - 1) % SIDE, pl.ds(2 * g, 2)],
            occ_all.at[-sign * d % SIDE, pl.ds(2 * g, 2)],
            occ_ring_send,
            occ_ring_recv.at[way, 2 * (d - 1) + g if d < 4 else 6],
            at(sign, 0),
        )

    def occ_step(d):
        for g in range(2):
            for way in range(2):
                if d == 4 and g != way:
                    continue
                piece = occ_all.at[(2 * way - 1) * d % SIDE, pl.ds(2 * g, 2)]
                slot = occ_ring_recv.at[way, 2 * (d - 1) + g if d < 4 else 6]
                remote(piece, piece, occ_ring_send, slot, at(1, 0)).wait_recv()
                if d < 3 or (d == 3 and g == way):
                    occ_ring(way, d + 1, g)

    def swap(j):
        pair = pl.ds(pl.multiple_of(jb * 2 * TILE, 2 * TILE), 2 * TILE)
        for i in FAR:
            send(strips.at[j, i, :, pair], landed.at[-i % SIDE, j], swap_send.at[0], swap_recv.at[0], at(i, 0))
        landed[0, j] = strips[j, 0, :, pair]

    def fill(i, carry):
        target = lax.broadcasted_iota(jnp.int32, (256, WIDE), 1)
        target = (target % 128) * RB + target // 128
        row = lax.broadcasted_iota(jnp.int32, (256, WIDE), 0) + i * 256
        perm[pl.ds(pl.multiple_of(i * 256, 256), 256), :] = jnp.where(row == target, 1.0, 0.0).astype(BF16)
        return carry

    def part(j):
        apart = jnp.dot(strips[j].reshape(128, WIDE), perm[...], preferred_element_type=F32).astype(BF16)
        for i in range(SIDE):
            for q in range(RB):
                left_side[j, q * ROWS : (q + 1) * ROWS, i * 128 : (i + 1) * 128] = apart[
                    i * ROWS : (i + 1) * ROWS, q * 128 : (q + 1) * 128
                ]

    place = [((par + j) % 2) * HALF + abs_b[j] // 2 for j in range(SIDE)]

    def contract(j):
        product = jnp.dot(left_side[j], vir_all[...].reshape(ORBS, 128), preferred_element_type=F32).astype(BF16)
        for q in range(RB):
            mixed[rows_of(place[j]), q * 128 : (q + 1) * 128] = product[q * ROWS : (q + 1) * ROWS]

    for m in (2, 1, 3):
        send(occ_all.at[0, 0], occ_all.at[0, -m % HALF], occ_one_send, occ_one_recv.at[-m % HALF // 2], at(0, 2 * m))
    for u in range(SUBS):
        for way in range(2):
            strip_ring(way, 1, u)
    swap(0)
    lax.fori_loop(0, WIDE // 256, fill, 0)

    blocks = vir_all.at[0, pl.ds(0, SIDE - 1)]
    remote(blocks, blocks, vir_send.at[0], vir_recv.at[0], at(0, 1)).wait()
    for i in FAR:
        send(vir_all.at[0], vir_all.at[-i % SIDE], vir_send.at[1], vir_recv.at[1], at(i, 0))

    def occ_begin():
        for g in range(2):
            blocks = occ_all.at[0, pl.ds(2, 2)] if g else occ_all.at[0, pl.ds(1, 1)]
            remote(blocks, blocks, occ_one_send, occ_one_recv.at[g], at(0, 1)).wait_recv()
            for way in range(2):
                occ_ring(way, 1, g)

    def vir_end():
        chunks = vir_all.at[pl.ds(0, SIDE - 1)]
        remote(chunks, chunks, vir_send.at[1], vir_recv.at[1], at(1, 0)).wait()

    def run(*steps):
        return [functools.partial(*step) for step in steps]

    work = {
        (1, 0): run((part, 0)),
        (1, 2): run((occ_begin,)),
        (2, 0): run((swap, 1), (swap, 7)),
        (2, 1): run((part, 1)),
        (2, 2): run((part, 7)),
        (2, 3): run((occ_step, 1)),
        (3, 0): run((swap, 2), (swap, 6), (vir_end,), (contract, 0)),
        (3, 1): run((part, 2), (contract, 1)),
        (3, 2): run((part, 6), (contract, 7)),
        (3, 3): run((occ_step, 2), (contract, 2), (contract, 6)),
        (4, 0): run((swap, 3), (swap, 5), (part, 3), (contract, 3)),
        (4, 1): run((part, 5), (contract, 5)),
    }
    for d in range(1, 5):
        for u in range(SUBS if d < 4 else SUBS // 2):
            for way in range(2):
                sub = u if d < 4 else u + way * SUBS // 2
                strip_wait(way, d, sub)
                if d < 3 or (d == 3 and u // (SUBS // 2) == way):
                    strip_ring(way, d + 1, sub)
            for step in work.get((d, u), ()):
                step()
    swap(4)
    part(4)
    contract(4)

    merged[...] = lax.dot_general(
        mixed[...], perm[...], (((1,), (1,)), ((), ())), preferred_element_type=F32
    ).astype(BF16)

    for i in FAR + [0]:
        for own in (False, True):
            if not (own and i == 0):
                parity = par if own else 1 - par
                send(
                    merged.at[rows_of(parity, 64), tile_of(abs_a[i])],
                    vir_land.at[par * SIDE + -i % SIDE],
                    swap_send.at[1],
                    swap_recv.at[1],
                    at(i, 0) if own else at_mate(i),
                )
    vir_land[par * SIDE] = merged[rows_of(par, 64), tile_of(a0)]

    for j in FAR:
        send(merged.at[rows_of(place[j])], vir_back.at[-j % SIDE], swap_send.at[2], swap_recv.at[2], at(0, j))
    occ_step(3)
    pieces = landed.at[pl.ds(0, SIDE - 1)]
    remote(pieces, pieces, swap_send.at[0], swap_recv.at[0], at(1, 0)).wait()
    for i in range(SIDE):
        for j in range(SIDE):
            both[rows_of(nat(i, j)), :] = landed[i, j]

    turn = [lax.rem(jb + m, HALF) for m in range(HALF)]

    def put_occ(i):
        product = jnp.dot(occ_all[i].reshape(64, ORBS), both[...], preferred_element_type=F32).astype(BF16)
        for m in range(HALF):
            occ_pair[rows_of(i * HALF + turn[m]), :] = product[m * ROWS : (m + 1) * ROWS]

    for i in (0, 1, 7, 2, 6, 3, 5):
        put_occ(i)
    occ_step(4)
    put_occ(4)
    occ_two[...] = occ_pair[:, tile_of(1 - par)]

    most = vir_land.at[pl.ds(0, 2 * SIDE - 1)]
    remote(most, most, swap_send.at[1], swap_recv.at[1], at(1, 0)).wait()

    gram = jnp.zeros((TILE, TILE), F32)
    for c in range(2):
        mine = occ_pair[:, c * TILE : (c + 1) * TILE]
        theirs = vir_land[c * SIDE : (c + 1) * SIDE].reshape(512, TILE)
        gram += lax.dot_general(mine, theirs, (((0,), (0,)), ((), ())), preferred_element_type=F32)
    row = lax.broadcasted_iota(jnp.int32, (TILE, TILE), 0)
    col = lax.broadcasted_iota(jnp.int32, (TILE, TILE), 1)
    gram = jnp.where(row // RB == col // RB, gram, 0.0)
    share = jnp.sum(gram.reshape(ROWS, RB, TILE), axis=0)

    def fold(values):
        for shift in (8, 16, 32, 64):
            values = values + pltpu.roll(values, shift, 1)
        return values

    spot = lax.broadcasted_iota(jnp.int32, (RB, TILE), 1) // RB == lax.broadcasted_iota(jnp.int32, (RB, TILE), 0)
    share = jnp.sum(jnp.where(spot, fold(share), 0.0), axis=0, keepdims=True)
    shares[pl.ds(grid_ix, 1), :] = share
    line = shares.at[pl.ds(grid_ix, 1)]
    for i in FAR + [0]:
        for j in FAR + [0]:
            if (i, j) != (0, 0):
                send(line, line, chi_send.at[0], chi_recv.at[0], at(i, j))

    pair_occ = remote(occ_two, occ_back, swap_send.at[3], swap_recv.at[3], at_mate(0))
    pair_occ.start()
    for a in range(SIDE):
        vir_out[0, :, tile_of(a * sa + part_b[0])] = merged[rows_of(place[0]), a * TILE : (a + 1) * TILE]
    for i in range(SIDE):
        for m in range(HALF):
            rows = rows_of(part_a[i] + (2 * m + par) * sb)
            occ_out[0, rows, :] = occ_pair[(i * HALF + m) * ROWS : (i * HALF + m + 1) * ROWS, tile_of(par)]
    for piece, sem in (
        (occ_all.at[0, pl.ds(0, HALF - 1)], occ_one_send),
        (occ_all.at[pl.ds(0, SIDE - 1)], occ_ring_send),
        (strips.at[pl.ds(0, SIDE - 1)], strip_send),
    ):
        remote(piece, piece, sem, io_sem.at[0], at(0, 1)).wait_send()

    lines = shares.at[pl.ds(0, PLANE - 1)]
    remote(lines, lines, chi_send.at[0], chi_recv.at[0], at(0, 1)).wait()
    shares_rep[pl.ds(rep_ix, 1), :] = jnp.sum(shares[...], axis=0, keepdims=True)
    line = shares_rep.at[pl.ds(rep_ix, 1)]
    for i in range(1, SIDE):
        send(line, line, chi_send.at[1], chi_recv.at[1], (grid_ix, around(rep_ix, i)))
    blocks = vir_back.at[pl.ds(0, SIDE - 1)]
    remote(blocks, blocks, swap_send.at[2], swap_recv.at[2], at(0, 1)).wait()
    for j in range(1, SIDE):
        for a in range(SIDE):
            vir_out[0, :, tile_of(a * sa + part_b[j])] = vir_back[j, :, a * TILE : (a + 1) * TILE]
    pair_occ.wait()
    for i in range(SIDE):
        for m in range(HALF):
            rows = rows_of(part_a[i] + (2 * m + 1 - par) * sb)
            occ_out[0, rows, :] = occ_back[(i * HALF + m) * ROWS : (i * HALF + m + 1) * ROWS]
    lines = shares_rep.at[pl.ds(0, SIDE - 1)]
    remote(lines, lines, chi_send.at[1], chi_recv.at[1], (grid_ix, around(rep_ix, 1))).wait()
    share = jnp.sum(shares_rep[...], axis=0, keepdims=True) * scale
    share = fold(jnp.where(spot, jnp.broadcast_to(share, (RB, TILE)), 0.0))
    chi_out[...] = share[:, :RB]


def write_out(occ_ref, vir_ref, chi_ref, occ_out, vir_out, chi_out, sems):
    copies = [
        pltpu.make_async_copy(src, dst, sems.at[i])
        for i, (src, dst) in enumerate(((occ_ref, occ_out), (vir_ref, vir_out), (chi_ref, chi_out)))
    ]
    for copy in copies:
        copy.start()
    for copy in copies:
        copy.wait()


def per_device(b_tensor, green_occ, green_vir, b_pattern, g_pattern):
    scale = -1.0 / (ORBS * math.sqrt(lax.axis_size("rep")))
    vmem = pl.BlockSpec(memory_space=pltpu.VMEM)
    hbm = pl.BlockSpec(memory_space=pltpu.HBM)
    dma = pltpu.SemaphoreType.DMA
    shapes = (
        jax.ShapeDtypeStruct((1, ORBS, TILE), BF16),
        jax.ShapeDtypeStruct((1, ROWS, ORBS * RB), BF16),
        jax.ShapeDtypeStruct((RB, RB), F32),
    )
    arguments = [
        pltpu.with_memory_space_constraint(t, pltpu.HBM)
        for t in (b_tensor, green_occ, green_vir, b_pattern, g_pattern)
    ]
    results = pl.pallas_call(
        functools.partial(kernel, scale),
        out_shape=shapes,
        in_specs=[hbm] * 5,
        out_specs=(vmem, vmem, vmem),
        scratch_shapes=[
            pltpu.VMEM(b_tensor.shape, BF16),
            pltpu.VMEM(green_occ.shape, BF16),
            pltpu.VMEM(green_vir.shape, BF16),
            pltpu.SMEM(b_pattern.shape, jnp.int32),
            pltpu.SMEM(g_pattern.shape, jnp.int32),
            pltpu.VMEM((SIDE, ROWS, 128), BF16),
            pltpu.VMEM((SIDE, SIDE, ROWS, 128), BF16),
            pltpu.VMEM((SIDE, HALF, ROWS, ORBS), BF16),
            pltpu.VMEM((SIDE, SIDE, ROWS, WIDE), BF16),
            pltpu.VMEM((SIDE, 128, ORBS), BF16),
            pltpu.VMEM((SIDE, SIDE, ROWS, 2 * TILE), BF16),
            pltpu.VMEM((ORBS, 2 * TILE), BF16),
            pltpu.VMEM((WIDE, WIDE), BF16),
            pltpu.VMEM((128, WIDE), BF16),
            pltpu.VMEM((128, WIDE), BF16),
            pltpu.VMEM((2 * SIDE, 64, TILE), BF16),
            pltpu.VMEM((SIDE, ROWS, WIDE), BF16),
            pltpu.VMEM((512, 2 * TILE), BF16),
            pltpu.VMEM((512, TILE), BF16),
            pltpu.VMEM((512, TILE), BF16),
            pltpu.VMEM((PLANE, TILE), F32),
            pltpu.VMEM((SIDE, TILE), F32),
            dma((5,)),
            dma((2,)),
            dma((2,)),
            dma,
            dma((2,)),
            dma,
            dma((2, 7)),
            dma,
            dma((2, 3 * SUBS + SUBS // 2)),
            dma((4,)),
            dma((4,)),
            dma((2,)),
            dma((2,)),
        ],
        compiler_params=pltpu.CompilerParams(
            collective_id=0, has_side_effects=True, vmem_limit_bytes=40 * 1024 * 1024
        ),
        cost_estimate=pl.CostEstimate(flops=600_000_000, bytes_accessed=1_200_000, transcendentals=0),
    )(*arguments)
    return pl.pallas_call(
        write_out,
        out_shape=shapes,
        in_specs=[vmem] * 3,
        out_specs=(hbm,) * 3,
        scratch_shapes=[dma((3,))],
        compiler_params=pltpu.CompilerParams(has_side_effects=True),
    )(*results)


def solution(mesh):
    return jax.shard_map(
        per_device,
        mesh=mesh,
        in_specs=(
            P("rep", "grid", None),
            P("rep", "grid", None),
            P("rep", "grid", None),
            P("rep", None, None),
            P("rep", None, None),
        ),
        out_specs=(P("rep", None, "grid"), P("rep", "grid", None), P()),
        check_vma=False,
    )
```

time: 308 us -> 69.1 us (0.22)
  waiting for transfers between devices: 132 us -> 0 us
  blocking collectives: 99 us -> 0 us
  Pallas kernels: 0 us -> 66.3 us
  starting transfers between devices: 25.6 us -> 0 us
  local copies, waits for them, and re-layouts: 20.9 us -> 1.97 us
  between operations: 14.1 us -> 0.65 us
  matrix products: 12.7 us -> 0 us
  other arithmetic: 3.73 us -> 0 us
    all_gather x2 -> x0, waiting for transfers between devices: 131 us -> none  [the longest x1 68.8 us: per_device(): lax.all_gather(occ_piece, 'grid', axis=0, tiled=True)]
    psum x1 -> x0, blocking collectives: 99 us -> none  [per_device(): chi = lax.psum(chi_part, ('grid', 'rep')) * scale]
    pallas_call x0 -> x2, Pallas kernels: none -> 66.3 us  [the longest x1 64.5 us: per_device(): pl.pallas_call(functools.partial(kernel, scale), out_shape=shapes, in_spe...]
    all_to_all x2 -> x0, starting transfers between devices: 25.5 us -> none  [the longest x1 17.1 us: per_device(): lax.all_to_all(flattened, 'grid', split_axis=1, concat_axis=0, tiled=True)]
    dot_general x5 -> x0, matrix products: 12.7 us -> none  [the longest x1 4.69 us: per_device(): lax.dot_general(occ_cols.reshape(-1, functions), vir_cols.reshape(-1, fun...]
    reshape x2 -> x0, local copies, waits for them, and re-layouts: 11.5 us -> none  [the longest x1 5.76 us: per_device(): occ_cols.reshape(-1, functions)]
    mul x3 -> x0, other arithmetic: 3.72 us -> none  [the longest x2 3.12 us: per_device(): b_tensor[0].reshape(rows_local, rows_all, functions)]
  transfers between devices with their start and end apart: 4 -> 0, of which waited for: 2 -> 0; matrix products, arithmetic and copies ran while one was open for 8% -> 0% of each run, Pallas kernels for 0% -> 0%
where the time goes in v3:
time: 69.1 us; the launch traced here: 68.9 us
  Pallas kernels  66.3 us (96%)
  local copies, waits for them, and re-layouts  1.97 us (3%)
    pallas_call x1, Pallas kernels, per_device(): pl.pallas_call(functools.partial(kernel, scale), out_shape=shapes, in_spe...  64.5 us
    unnamed x6, local copies, waits for them, and re-layouts  1.97 us
    pallas_call x1, Pallas kernels, per_device(): pl.pallas_call(write_out, out_shape=shapes, in_specs=[vmem] * 3, out_spec...  1.84 us

profile of v3, /device:TPU:1, one launch (start us, length us, event | category | flops | bytes accessed | tf_op | source)
XLA Modules:
  0.0 68.9 jit_solution(13183972031805762290)
XLA Ops:
  0.6 64.5 %shard_map.76 = (bf16[1,1024,128]{2,1,0:T(8,128)(2,1)S(1)}, bf16[1,16,8192]{2,1,0:T(8,128)(2,1)S(1)}, f32[8,8]{1,0:T(8,128)S(1)}) custom-call(bf16[1,16,8192]{2,1,0:T(8,128)(2,1)} %b_hbm.1, bf16[1,16,1024]{2,1,0:T(8,128)(2,1)} %occ_hbm.1, bf16[1,16,1024]{2,1,0:T(8,128)(2,1)} %vir_hbm.1, s32[1,16,16]{2,1,0:T(8,128)} %bp_hbm.1, s32[1,16,16]{2,1,0:T(8,128)} %gp_hbm.1), custom_call_target="tpu_custom_call" | custom-call | flops 600000000 | bytes 1200000 | tf_op jit(solution)/shard_map/pallas_call | solution.py:418
  65.1 0.0 copy-start
  65.1 0.7 copy-done
  65.8 0.0 copy-start.1
  65.8 0.7 copy-done.1
  66.5 0.0 copy-start.2
  66.5 0.6 copy-done.2
  67.1 1.8 %shard_map.77 = (bf16[1,1024,128]{2,1,0:T(8,128)(2,1)}, bf16[1,16,8192]{2,1,0:T(8,128)(2,1)}, f32[8,8]{1,0:T(8,128)}) custom-call(bf16[1,1024,128]{2,1,0:T(8,128)(2,1)} %copy-done, bf16[1,16,8192]{2,1,0:T(8,128)(2,1)} %copy-done.1, f32[8,8]{1,0:T(8,128)} %copy-done.2), custom_call_target="tpu_custom_call" | custom-call | tf_op jit(solution)/shard_map/pallas_call | solution.py:465
Async XLA Ops:
  65.1 0.7 %copy-start = (bf16[1,1024,128]{2,1,0:T(8,128)(2,1)}, bf16[1,1024,128]{2,1,0:T(8,128)(2,1)S(1)}, u32[]{:S(2)}) copy-start(bf16[1,1024,128]{2,1,0:T(8,128)(2,1)S(1)} %get-tuple-element.6.occ_ref) | copy-start | bytes 786436
  65.8 0.7 %copy-start.1 = (bf16[1,16,8192]{2,1,0:T(8,128)(2,1)}, bf16[1,16,8192]{2,1,0:T(8,128)(2,1)S(1)}, u32[]{:S(2)}) copy-start(bf16[1,16,8192]{2,1,0:T(8,128)(2,1)S(1)} %get-tuple-element.7.vir_ref) | copy-start | bytes 786436
  66.5 0.6 copy-start.2

commit v4 on v3

--- a/solution.py
+++ b/solution.py
@@ -242,8 +242,27 @@
 
     blocks = vir_all.at[0, pl.ds(0, SIDE - 1)]
     remote(blocks, blocks, vir_send.at[0], vir_recv.at[0], at(0, 1)).wait()
-    for i in FAR:
-        send(vir_all.at[0], vir_all.at[-i % SIDE], vir_send.at[1], vir_recv.at[1], at(i, 0))
+    def vir_ring(way, d):
+        sign = 1 - 2 * way
+        part_of = slice(None) if d < 4 else pl.ds(way * HALF, HALF)
+        send(
+            vir_all.at[-sign * (d - 1) % SIDE, part_of],
+            vir_all.at[-sign * d % SIDE, part_of],
+            vir_send.at[1],
+            vir_recv.at[2 * d - 1 + way],
+            at(sign, 0),
+        )
+
+    def vir_step(d):
+        for way in range(2):
+            part_of = slice(None) if d < 4 else pl.ds(way * HALF, HALF)
+            chunk = vir_all.at[(2 * way - 1) * d % SIDE, part_of]
+            remote(chunk, chunk, vir_send.at[1], vir_recv.at[2 * d - 1 + way], at(1, 0)).wait_recv()
+            if d < 4:
+                vir_ring(way, d + 1)
+
+    for way in range(2):
+        vir_ring(way, 1)
 
     def occ_begin():
         for g in range(2):
@@ -253,8 +272,9 @@
                 occ_ring(way, 1, g)
 
     def vir_end():
+        vir_step(4)
         chunks = vir_all.at[pl.ds(0, SIDE - 1)]
-        remote(chunks, chunks, vir_send.at[1], vir_recv.at[1], at(1, 0)).wait()
+        remote(chunks, chunks, vir_send.at[1], vir_recv.at[1], at(1, 0)).wait_send()
 
     def run(*steps):
         return [functools.partial(*step) for step in steps]
@@ -262,16 +282,16 @@
     work = {
         (1, 0): run((part, 0)),
         (1, 2): run((occ_begin,)),
-        (2, 0): run((swap, 1), (swap, 7)),
+        (2, 0): run((vir_step, 1), (swap, 1), (swap, 7)),
         (2, 1): run((part, 1)),
         (2, 2): run((part, 7)),
-        (2, 3): run((occ_step, 1)),
-        (3, 0): run((swap, 2), (swap, 6), (vir_end,), (contract, 0)),
-        (3, 1): run((part, 2), (contract, 1)),
-        (3, 2): run((part, 6), (contract, 7)),
-        (3, 3): run((occ_step, 2), (contract, 2), (contract, 6)),
-        (4, 0): run((swap, 3), (swap, 5), (part, 3), (contract, 3)),
-        (4, 1): run((part, 5), (contract, 5)),
+        (2, 3): run((vir_step, 2), (occ_step, 1)),
+        (3, 0): run((swap, 2), (swap, 6)),
+        (3, 1): run((vir_step, 3), (part, 2)),
+        (3, 2): run((part, 6)),
+        (3, 3): run((occ_step, 2),),
+        (4, 0): run((swap, 3), (swap, 5), (part, 3)),
+        (4, 1): run((part, 5), (vir_end,), (contract, 0), (contract, 1), (contract, 7), (contract, 2), (contract, 6), (contract, 3), (contract, 5)),
     }
     for d in range(1, 5):
         for u in range(SUBS if d < 4 else SUBS // 2):
@@ -345,15 +365,23 @@
 
     spot = lax.broadcasted_iota(jnp.int32, (RB, TILE), 1) // RB == lax.broadcasted_iota(jnp.int32, (RB, TILE), 0)
     share = jnp.sum(jnp.where(spot, fold(share), 0.0), axis=0, keepdims=True)
-    shares[pl.ds(grid_ix, 1), :] = share
+    shares_rep[pl.ds(rep_ix, 1), :] = share
+    line = shares_rep.at[pl.ds(rep_ix, 1)]
+    for i in range(1, SIDE):
+        send(line, line, chi_send.at[1], chi_recv.at[1], (grid_ix, around(rep_ix, i)))
+
+    pair_occ = remote(occ_two, occ_back, swap_send.at[3], swap_recv.at[3], at_mate(0))
+    pair_occ.start()
+
+    lines = shares_rep.at[pl.ds(0, SIDE - 1)]
+    remote(lines, lines, chi_send.at[1], chi_recv.at[1], (grid_ix, around(rep_ix, 1))).wait()
+    shares[pl.ds(grid_ix, 1), :] = jnp.sum(shares_rep[...], axis=0, keepdims=True)
     line = shares.at[pl.ds(grid_ix, 1)]
     for i in FAR + [0]:
         for j in FAR + [0]:
             if (i, j) != (0, 0):
                 send(line, line, chi_send.at[0], chi_recv.at[0], at(i, j))
 
-    pair_occ = remote(occ_two, occ_back, swap_send.at[3], swap_recv.at[3], at_mate(0))
-    pair_occ.start()
     for a in range(SIDE):
         vir_out[0, :, tile_of(a * sa + part_b[0])] = merged[rows_of(place[0]), a * TILE : (a + 1) * TILE]
     for i in range(SIDE):
@@ -367,12 +395,6 @@
     ):
         remote(piece, piece, sem, io_sem.at[0], at(0, 1)).wait_send()
 
-    lines = shares.at[pl.ds(0, PLANE - 1)]
-    remote(lines, lines, chi_send.at[0], chi_recv.at[0], at(0, 1)).wait()
-    shares_rep[pl.ds(rep_ix, 1), :] = jnp.sum(shares[...], axis=0, keepdims=True)
-    line = shares_rep.at[pl.ds(rep_ix, 1)]
-    for i in range(1, SIDE):
-        send(line, line, chi_send.at[1], chi_recv.at[1], (grid_ix, around(rep_ix, i)))
     blocks = vir_back.at[pl.ds(0, SIDE - 1)]
     remote(blocks, blocks, swap_send.at[2], swap_recv.at[2], at(0, 1)).wait()
     for j in range(1, SIDE):
@@ -383,22 +405,11 @@
         for m in range(HALF):
             rows = rows_of(part_a[i] + (2 * m + 1 - par) * sb)
             occ_out[0, rows, :] = occ_back[(i * HALF + m) * ROWS : (i * HALF + m + 1) * ROWS]
-    lines = shares_rep.at[pl.ds(0, SIDE - 1)]
-    remote(lines, lines, chi_send.at[1], chi_recv.at[1], (grid_ix, around(rep_ix, 1))).wait()
-    share = jnp.sum(shares_rep[...], axis=0, keepdims=True) * scale
+    lines = shares.at[pl.ds(0, PLANE - 1)]
+    remote(lines, lines, chi_send.at[0], chi_recv.at[0], at(0, 1)).wait()
+    share = jnp.sum(shares[...], axis=0, keepdims=True) * scale
     share = fold(jnp.where(spot, jnp.broadcast_to(share, (RB, TILE)), 0.0))
     chi_out[...] = share[:, :RB]
-
-
-def write_out(occ_ref, vir_ref, chi_ref, occ_out, vir_out, chi_out, sems):
-    copies = [
-        pltpu.make_async_copy(src, dst, sems.at[i])
-        for i, (src, dst) in enumerate(((occ_ref, occ_out), (vir_ref, vir_out), (chi_ref, chi_out)))
-    ]
-    for copy in copies:
-        copy.start()
-    for copy in copies:
-        copy.wait()
 
 
 def per_device(b_tensor, green_occ, green_vir, b_pattern, g_pattern):
@@ -415,7 +426,7 @@
         pltpu.with_memory_space_constraint(t, pltpu.HBM)
         for t in (b_tensor, green_occ, green_vir, b_pattern, g_pattern)
     ]
-    results = pl.pallas_call(
+    return pl.pallas_call(
         functools.partial(kernel, scale),
         out_shape=shapes,
         in_specs=[hbm] * 5,
@@ -445,7 +456,7 @@
             pltpu.VMEM((SIDE, TILE), F32),
             dma((5,)),
             dma((2,)),
-            dma((2,)),
+            dma((9,)),
             dma,
             dma((2,)),
             dma,
@@ -462,14 +473,6 @@
         ),
         cost_estimate=pl.CostEstimate(flops=600_000_000, bytes_accessed=1_200_000, transcendentals=0),
     )(*arguments)
-    return pl.pallas_call(
-        write_out,
-        out_shape=shapes,
-        in_specs=[vmem] * 3,
-        out_specs=(hbm,) * 3,
-        scratch_shapes=[dma((3,))],
-        compiler_params=pltpu.CompilerParams(has_side_effects=True),
-    )(*results)
 
 
 def solution(mesh):

time: 69.1 us -> 64.6 us (0.935)
  Pallas kernels: 66.3 us -> 61.8 us
    pallas_call x1, Pallas kernels: 64.5 us -> 61.8 us  [per_device(): pl.pallas_call(functools.partial(kernel, scale), out_shape=shapes, in_spe...]
    pallas_call x1 -> x0, Pallas kernels: 1.84 us -> none  [per_device(): pl.pallas_call(write_out, out_shape=shapes, in_specs=[vmem] * 3, out_spec...]
    unnamed x6 -> x3, local copies, waits for them, and re-layouts: 1.97 us -> 2 us
where the time goes in v4:
time: 64.6 us; the launch traced here: 64.4 us
  Pallas kernels  61.8 us (96%)
  local copies, waits for them, and re-layouts  2 us (3%)
    pallas_call x1, Pallas kernels, per_device(): pl.pallas_call(functools.partial(kernel, scale), out_shape=shapes, in_spe...  61.8 us
    unnamed x3, local copies, waits for them, and re-layouts  2 us

profile of v4, /device:TPU:1, one launch (start us, length us, event | category | flops | bytes accessed | tf_op | source)
XLA Modules:
  0.0 64.4 jit_solution(2721458217548281662)
XLA Ops:
  0.6 61.8 %shard_map.76 = (bf16[1,1024,128]{2,1,0:T(8,128)(2,1)S(1)}, bf16[1,16,8192]{2,1,0:T(8,128)(2,1)S(1)}, f32[8,8]{1,0:T(8,128)S(1)}) custom-call(bf16[1,16,8192]{2,1,0:T(8,128)(2,1)} %b_hbm.1, bf16[1,16,1024]{2,1,0:T(8,128)(2,1)} %occ_hbm.1, bf16[1,16,1024]{2,1,0:T(8,128)(2,1)} %vir_hbm.1, s32[1,16,16]{2,1,0:T(8,128)} %bp_hbm.1, s32[1,16,16]{2,1,0:T(8,128)} %gp_hbm.1), custom_call_target="tpu_custom_call" | custom-call | flops 600000000 | bytes 1200000 | tf_op jit(solution)/shard_map/pallas_call | solution.py:429
  62.4 0.7 %copy.11 = bf16[1,1024,128]{2,1,0:T(8,128)(2,1)} copy(bf16[1,1024,128]{2,1,0:T(8,128)(2,1)S(1)} %get-tuple-element.6) | data formatting | bytes 524288
  63.1 0.7 %copy.12 = bf16[1,16,8192]{2,1,0:T(8,128)(2,1)} copy(bf16[1,16,8192]{2,1,0:T(8,128)(2,1)S(1)} %get-tuple-element.7) | data formatting | bytes 524288
  63.8 0.6 copy.13

commit v5 on v4

--- a/solution.py
+++ b/solution.py
@@ -26,6 +26,7 @@
 
 
 FAR = [4, 5, 3, 6, 2, 7, 1]
+ORDER = [0, 1, 7, 2, 6, 3, 5, 4]
 SUBS = 4
 
 
@@ -225,12 +226,32 @@
                     i * ROWS : (i + 1) * ROWS, q * 128 : (q + 1) * 128
                 ]
 
-    place = [((par + j) % 2) * HALF + abs_b[j] // 2 for j in range(SIDE)]
-
     def contract(j):
         product = jnp.dot(left_side[j], vir_all[...].reshape(ORBS, 128), preferred_element_type=F32).astype(BF16)
+        row = ORDER.index(j) * ROWS
         for q in range(RB):
-            mixed[rows_of(place[j]), q * 128 : (q + 1) * 128] = product[q * ROWS : (q + 1) * ROWS]
+            mixed[row : row + ROWS, q * 128 : (q + 1) * 128] = product[q * ROWS : (q + 1) * ROWS]
+
+    def finish(*js):
+        first = ORDER.index(js[0]) * ROWS
+        rows = slice(first, first + len(js) * ROWS)
+        merged[rows] = lax.dot_general(
+            mixed[rows], perm[...], (((1,), (1,)), ((), ())), preferred_element_type=F32
+        ).astype(BF16)
+        for j in js:
+            row = ORDER.index(j) * ROWS
+            line = rows_of(abs_b[j] // 2)
+            for i in FAR + [0]:
+                piece = merged.at[row : row + ROWS, tile_of(abs_a[i])]
+                land = vir_land.at[par * SIDE + -i % SIDE, line]
+                if j % 2 == 1 or i != 0:
+                    send(piece, land, swap_send.at[1], swap_recv.at[1], at_mate(i) if j % 2 else at(i, 0))
+            if j % 2 == 0:
+                vir_land[par * SIDE, line] = merged[row : row + ROWS, tile_of(a0)]
+        for j in js:
+            if j != 0:
+                row = ORDER.index(j) * ROWS
+                send(merged.at[row : row + ROWS], vir_back.at[-j % SIDE], swap_send.at[2], swap_recv.at[2], at(0, j))
 
     for m in (2, 1, 3):
         send(occ_all.at[0, 0], occ_all.at[0, -m % HALF], occ_one_send, occ_one_recv.at[-m % HALF // 2], at(0, 2 * m))
@@ -242,27 +263,25 @@
 
     blocks = vir_all.at[0, pl.ds(0, SIDE - 1)]
     remote(blocks, blocks, vir_send.at[0], vir_recv.at[0], at(0, 1)).wait()
-    def vir_ring(way, d):
-        sign = 1 - 2 * way
-        part_of = slice(None) if d < 4 else pl.ds(way * HALF, HALF)
-        send(
-            vir_all.at[-sign * (d - 1) % SIDE, part_of],
-            vir_all.at[-sign * d % SIDE, part_of],
-            vir_send.at[1],
-            vir_recv.at[2 * d - 1 + way],
-            at(sign, 0),
-        )
-
-    def vir_step(d):
+    for d in (2, 1):
         for way in range(2):
-            part_of = slice(None) if d < 4 else pl.ds(way * HALF, HALF)
-            chunk = vir_all.at[(2 * way - 1) * d % SIDE, part_of]
-            remote(chunk, chunk, vir_send.at[1], vir_recv.at[2 * d - 1 + way], at(1, 0)).wait_recv()
-            if d < 4:
-                vir_ring(way, d + 1)
-
-    for way in range(2):
-        vir_ring(way, 1)
+            step = d * (1 - 2 * way)
+            send(vir_all.at[0], vir_all.at[-step % SIDE], vir_send.at[1], vir_recv.at[1 if d == 1 else 2 + way], at(step, 0))
+
+    def vir_relay():
+        for way in range(2):
+            sign = 1 - 2 * way
+            chunk = vir_all.at[-2 * sign % SIDE]
+            remote(chunk, chunk, vir_send.at[1], vir_recv.at[2 + way], at(1, 0)).wait_recv()
+            half = pl.ds(way * HALF, HALF)
+            send(
+                vir_all.at[-2 * sign % SIDE, half],
+                vir_all.at[HALF, half],
+                vir_send.at[1],
+                vir_recv.at[1],
+                at(2 * sign, 0),
+            )
+            send(chunk, vir_all.at[-3 * sign % SIDE], vir_send.at[1], vir_recv.at[1], at(sign, 0))
 
     def occ_begin():
         for g in range(2):
@@ -272,7 +291,8 @@
                 occ_ring(way, 1, g)
 
     def vir_end():
-        vir_step(4)
+        chunks = vir_all.at[pl.ds(0, 5)]
+        remote(chunks, chunks, vir_send.at[1], vir_recv.at[1], at(1, 0)).wait_recv()
         chunks = vir_all.at[pl.ds(0, SIDE - 1)]
         remote(chunks, chunks, vir_send.at[1], vir_recv.at[1], at(1, 0)).wait_send()
 
@@ -280,18 +300,19 @@
         return [functools.partial(*step) for step in steps]
 
     work = {
-        (1, 0): run((part, 0)),
+        (1, 0): run((part, 0,)),
         (1, 2): run((occ_begin,)),
-        (2, 0): run((vir_step, 1), (swap, 1), (swap, 7)),
-        (2, 1): run((part, 1)),
-        (2, 2): run((part, 7)),
-        (2, 3): run((vir_step, 2), (occ_step, 1)),
-        (3, 0): run((swap, 2), (swap, 6)),
-        (3, 1): run((vir_step, 3), (part, 2)),
-        (3, 2): run((part, 6)),
-        (3, 3): run((occ_step, 2),),
-        (4, 0): run((swap, 3), (swap, 5), (part, 3)),
-        (4, 1): run((part, 5), (vir_end,), (contract, 0), (contract, 1), (contract, 7), (contract, 2), (contract, 6), (contract, 3), (contract, 5)),
+        (1, 3): run((vir_relay,)),
+        (2, 0): run((swap, 1,), (swap, 7,)),
+        (2, 1): run((part, 1,)),
+        (2, 2): run((part, 7,)),
+        (2, 3): run((occ_step, 1,)),
+        (3, 0): run((swap, 2,), (swap, 6,)),
+        (3, 1): run((part, 2,), (vir_end,), (contract, 0,), (contract, 1,)),
+        (3, 2): run((part, 6,), (contract, 7,), (contract, 2,), (contract, 6,)),
+        (3, 3): run((occ_step, 2,), (finish, 0, 1, 7, 2, 6,)),
+        (4, 0): run((swap, 3,), (swap, 5,), (part, 3,), (contract, 3,)),
+        (4, 1): run((part, 5,), (contract, 5,), (finish, 3, 5,)),
     }
     for d in range(1, 5):
         for u in range(SUBS if d < 4 else SUBS // 2):
@@ -306,25 +327,7 @@
     part(4)
     contract(4)
 
-    merged[...] = lax.dot_general(
-        mixed[...], perm[...], (((1,), (1,)), ((), ())), preferred_element_type=F32
-    ).astype(BF16)
-
-    for i in FAR + [0]:
-        for own in (False, True):
-            if not (own and i == 0):
-                parity = par if own else 1 - par
-                send(
-                    merged.at[rows_of(parity, 64), tile_of(abs_a[i])],
-                    vir_land.at[par * SIDE + -i % SIDE],
-                    swap_send.at[1],
-                    swap_recv.at[1],
-                    at(i, 0) if own else at_mate(i),
-                )
-    vir_land[par * SIDE] = merged[rows_of(par, 64), tile_of(a0)]
-
-    for j in FAR:
-        send(merged.at[rows_of(place[j])], vir_back.at[-j % SIDE], swap_send.at[2], swap_recv.at[2], at(0, j))
+    finish(4)
     occ_step(3)
     pieces = landed.at[pl.ds(0, SIDE - 1)]
     remote(pieces, pieces, swap_send.at[0], swap_recv.at[0], at(1, 0)).wait()
@@ -383,7 +386,7 @@
                 send(line, line, chi_send.at[0], chi_recv.at[0], at(i, j))
 
     for a in range(SIDE):
-        vir_out[0, :, tile_of(a * sa + part_b[0])] = merged[rows_of(place[0]), a * TILE : (a + 1) * TILE]
+        vir_out[0, :, tile_of(a * sa + part_b[0])] = merged[:ROWS, a * TILE : (a + 1) * TILE]
     for i in range(SIDE):
         for m in range(HALF):
             rows = rows_of(part_a[i] + (2 * m + par) * sb)
@@ -456,7 +459,7 @@
             pltpu.VMEM((SIDE, TILE), F32),
             dma((5,)),
             dma((2,)),
-            dma((9,)),
+            dma((4,)),
             dma,
             dma((2,)),
             dma,

time: 64.6 us -> 63.8 us (0.988)
  Pallas kernels: 61.8 us -> 61 us
    pallas_call x1, Pallas kernels: 61.8 us -> 61 us  [per_device(): pl.pallas_call(functools.partial(kernel, scale), out_shape=shapes, in_spe...]
where the time goes in v5:
time: 63.8 us; the launch traced here: 63.7 us
  Pallas kernels  61 us (96%)
  local copies, waits for them, and re-layouts  2 us (3%)
  between operations  0.64 us (1%)
    pallas_call x1, Pallas kernels, per_device(): pl.pallas_call(functools.partial(kernel, scale), out_shape=shapes, in_spe...  61 us
    unnamed x3, local copies, waits for them, and re-layouts  2 us

profile of v5, /device:TPU:1, one launch (start us, length us, event | category | flops | bytes accessed | tf_op | source)
XLA Modules:
  0.0 63.7 jit_solution(5385505409441439375)
XLA Ops:
  0.6 61.0 %shard_map.76 = (bf16[1,1024,128]{2,1,0:T(8,128)(2,1)S(1)}, bf16[1,16,8192]{2,1,0:T(8,128)(2,1)S(1)}, f32[8,8]{1,0:T(8,128)S(1)}) custom-call(bf16[1,16,8192]{2,1,0:T(8,128)(2,1)} %b_hbm.1, bf16[1,16,1024]{2,1,0:T(8,128)(2,1)} %occ_hbm.1, bf16[1,16,1024]{2,1,0:T(8,128)(2,1)} %vir_hbm.1, s32[1,16,16]{2,1,0:T(8,128)} %bp_hbm.1, s32[1,16,16]{2,1,0:T(8,128)} %gp_hbm.1), custom_call_target="tpu_custom_call" | custom-call | flops 600000000 | bytes 1200000 | tf_op jit(solution)/shard_map/pallas_call | solution.py:432
  61.7 0.7 %copy.11 = bf16[1,1024,128]{2,1,0:T(8,128)(2,1)} copy(bf16[1,1024,128]{2,1,0:T(8,128)(2,1)S(1)} %get-tuple-element.6) | data formatting | bytes 524288
  62.4 0.7 %copy.12 = bf16[1,16,8192]{2,1,0:T(8,128)(2,1)} copy(bf16[1,16,8192]{2,1,0:T(8,128)(2,1)S(1)} %get-tuple-element.7) | data formatting | bytes 524288
  63.1 0.6 copy.13

commit v6 on v5

--- a/solution.py
+++ b/solution.py
@@ -150,6 +150,9 @@
         vir_own[b] = tiles[b].astype(BF16)
     vir_all[0, b0] = vir_own[b0]
 
+    pl.semaphore_wait(barrier, 3 * (SIDE - 1))
+    for j in FAR:
+        send(vir_own.at[abs_b[j]], vir_all.at[0, b0], vir_send.at[0], vir_recv.at[0], at(0, j))
     loads[2].wait()
     loads[3].wait()
     for m in range(2 * SIDE):
@@ -164,10 +167,6 @@
         cols = slice(t * 128, (t + 1) * 128)
         occ_all[0, 0, :, cols] = occ_ref[0, :, cols] * keeps[t].astype(BF16)
 
-    pl.semaphore_wait(barrier, 3 * (SIDE - 1))
-
-    for j in FAR:
-        send(vir_own.at[abs_b[j]], vir_all.at[0, b0], vir_send.at[0], vir_recv.at[0], at(0, j))
 
     def strip_ring(way, d, u):
         sign = 1 - 2 * way
@@ -374,7 +373,6 @@
         send(line, line, chi_send.at[1], chi_recv.at[1], (grid_ix, around(rep_ix, i)))
 
     pair_occ = remote(occ_two, occ_back, swap_send.at[3], swap_recv.at[3], at_mate(0))
-    pair_occ.start()
 
     lines = shares_rep.at[pl.ds(0, SIDE - 1)]
     remote(lines, lines, chi_send.at[1], chi_recv.at[1], (grid_ix, around(rep_ix, 1))).wait()
@@ -384,6 +382,7 @@
         for j in FAR + [0]:
             if (i, j) != (0, 0):
                 send(line, line, chi_send.at[0], chi_recv.at[0], at(i, j))
+    pair_occ.start()
 
     for a in range(SIDE):
         vir_out[0, :, tile_of(a * sa + part_b[0])] = merged[:ROWS, a * TILE : (a + 1) * TILE]

time: 63.8 us -> 64 us (level)
  no operation moved by 1% of the time
where the time goes in v6:
time: 64 us; the launch traced here: 63.8 us
  Pallas kernels  61.2 us (96%)
  local copies, waits for them, and re-layouts  2 us (3%)
  between operations  0.64 us (1%)
    pallas_call x1, Pallas kernels, per_device(): pl.pallas_call(functools.partial(kernel, scale), out_shape=shapes, in_spe...  61.2 us
    unnamed x3, local copies, waits for them, and re-layouts  2 us

profile of v6, /device:TPU:1, one launch (start us, length us, event | category | flops | bytes accessed | tf_op | source)
XLA Modules:
  0.0 63.8 jit_solution(11673105044500323621)
XLA Ops:
  0.6 61.2 %shard_map.76 = (bf16[1,1024,128]{2,1,0:T(8,128)(2,1)S(1)}, bf16[1,16,8192]{2,1,0:T(8,128)(2,1)S(1)}, f32[8,8]{1,0:T(8,128)S(1)}) custom-call(bf16[1,16,8192]{2,1,0:T(8,128)(2,1)} %b_hbm.1, bf16[1,16,1024]{2,1,0:T(8,128)(2,1)} %occ_hbm.1, bf16[1,16,1024]{2,1,0:T(8,128)(2,1)} %vir_hbm.1, s32[1,16,16]{2,1,0:T(8,128)} %bp_hbm.1, s32[1,16,16]{2,1,0:T(8,128)} %gp_hbm.1), custom_call_target="tpu_custom_call" | custom-call | flops 600000000 | bytes 1200000 | tf_op jit(solution)/shard_map/pallas_call | solution.py:431
  61.8 0.7 %copy.11 = bf16[1,1024,128]{2,1,0:T(8,128)(2,1)} copy(bf16[1,1024,128]{2,1,0:T(8,128)(2,1)S(1)} %get-tuple-element.6) | data formatting | bytes 524288
  62.5 0.7 %copy.12 = bf16[1,16,8192]{2,1,0:T(8,128)(2,1)} copy(bf16[1,16,8192]{2,1,0:T(8,128)(2,1)S(1)} %get-tuple-element.7) | data formatting | bytes 524288
  63.2 0.6 copy.13
